TPU v7x, 32 devices: a whole 2x2x4 slice. The times are simulated.
32 devices in a mesh: dp: 8 (over z, x), seq: 4 (over y, core).
Axes of the slice: x: 2, y: 2, z: 4, core: 2. Of those that a mesh axis runs over, the one named last changes fastest.
Arguments:
- hidden_in: bfloat16 [24576, 1024], P(('dp', 'seq')), may hold values from -6 to 6
- key_bias: float32 [8, 3072], P('dp', 'seq'), may hold values from -4 to 4
- w_qkv: bfloat16 [1024, 3072], P('dp'), may hold values from -0.1875 to 0.1875
- bias_q: bfloat16 [1024], P('dp'), may hold values from -3 to 3
- bias_v: bfloat16 [1024], P('dp'), may hold values from -0.75 to 0.75
- w_out: bfloat16 [1024, 1024], P('dp'), may hold values from -3 to 3
- bias_out: bfloat16 [1024], P('dp'), may hold values from -3 to 3
- gain_attn: bfloat16 [1024], P('dp'), may hold values from 0.25 to 1.75
- shift_attn: bfloat16 [1024], P('dp'), may hold values from -3 to 3
- w_up: bfloat16 [1024, 4096], P('dp'), may hold values from -0.1875 to 0.1875
- bias_up: bfloat16 [4096], P('dp'), may hold values from -3 to 3
- w_down: bfloat16 [4096, 1024], P('dp'), may hold values from -0.09375 to 0.09375
- bias_down: bfloat16 [1024], P('dp'), may hold values from -3 to 3
- gain_ffn: bfloat16 [1024], P('dp'), may hold values from 0.25 to 1.75
- shift_ffn: bfloat16 [1024], P('dp'), may hold values from -3 to 3
- grad_out: bfloat16 [24576, 1024], P(('dp', 'seq')), may hold values from -6 to 6
Outputs:
- output: bfloat16 [24576, 1024], P(('dp', 'seq'))
- grad_in: float32 [24576, 1024], P(('dp', 'seq'))
- grad_w_qkv: float32 [1024, 3072], P('dp')
- grad_bias_q: float32 [1024], P('dp')
- grad_bias_v: float32 [1024], P('dp')
- grad_w_out: float32 [1024, 1024], P('dp')
- grad_bias_out: float32 [1024], P('dp')
- grad_gain_attn: float32 [1024], P('dp')
- grad_shift_attn: float32 [1024], P('dp')
- grad_w_up: float32 [1024, 4096], P('dp')
- grad_bias_up: float32 [4096], P('dp')
- grad_w_down: float32 [4096, 1024], P('dp')
- grad_bias_down: float32 [1024], P('dp')
- grad_gain_ffn: float32 [1024], P('dp')
- grad_shift_ffn: float32 [1024], P('dp')
All inputs are finite; a program needn't handle non-finite values.
Results may differ from a plain program's by a relative error of at most 0.02.
Values may be sent and summed in bfloat16 or wider, within the bound.
A program may use at most 192 MiB of HBM per device.

v0:
```python
import jax
import jax.numpy as jnp
from jax import lax
from jax.sharding import PartitionSpec as P

HEAD_DIM = 64


norm_eps = 1e-05


def shortened(array):

    def short(part):
        return part.astype(jnp.bfloat16) if part.dtype == jnp.float32 else part

    return jax.tree.map(short, array)


def layer_norm(hidden, gain_vec, shift_vec):
    row_mean = jnp.mean(hidden, -1, keepdims=True)
    centered = hidden - row_mean
    row_var = jnp.mean(centered * centered, -1, keepdims=True)
    return centered * lax.rsqrt(row_var + norm_eps) * gain_vec + shift_vec


def gelu_exact(pre_act):
    return jax.nn.gelu(pre_act, approximate=False)


def matmul(left, right):
    return jnp.dot(left, right, preferred_element_type=jnp.float32)


def matmul_left(left, right):
    return lax.dot_general(
        left, right, (((0,), (0,)), ((), ())), preferred_element_type=jnp.float32
    )


def matmul_right(left, right):
    return lax.dot_general(
        left, right, (((1,), (1,)), ((), ())), preferred_element_type=jnp.float32
    )


def attend_forward(queries, keys_all, values_all, bias_row, score_scale):
    length, heads_loc, head_width = queries.shape
    block_rows = min(512, length)
    head_step = min(2, heads_loc)
    blocks = queries.reshape(length // block_rows, block_rows, heads_loc, head_width)

    def one_block(query_blk):
        pieces = []
        totals_list = []
        for start_head in range(0, heads_loc, head_step):
            part = slice(start_head, start_head + head_step)
            scores = (
                jnp.einsum(
                    "bhe,lhe->hbl",
                    query_blk[:, part],
                    keys_all[:, part],
                    preferred_element_type=jnp.float32,
                )
                * score_scale
                + bias_row
            )
            row_max = jnp.max(scores, -1, keepdims=True)
            expo = jnp.exp(scores - row_max)
            row_total = jnp.sum(expo, -1, keepdims=True)
            probs_low = (expo / row_total).astype(jnp.bfloat16)
            pieces.append(
                jnp.einsum(
                    "hbl,lhe->bhe",
                    probs_low,
                    values_all[:, part],
                    preferred_element_type=jnp.float32,
                )
            )
            totals_list.append((row_max + jnp.log(row_total))[..., 0])
        return (jnp.concatenate(pieces, 1).astype(jnp.bfloat16), jnp.concatenate(totals_list, 0))

    context, log_total = lax.map(one_block, blocks)
    return (context.reshape(length, heads_loc * head_width), log_total)


def attend_backward(queries, keys_all, values_all, bias_row, score_scale, log_total, context_grad):
    length, heads_loc, head_width = queries.shape
    block_rows = min(512, length)
    head_step = min(2, heads_loc)
    query_blocks = queries.reshape(length // block_rows, block_rows, heads_loc, head_width)
    grad_blocks = context_grad.reshape(length // block_rows, block_rows, heads_loc, head_width)

    def one_block(carry_in, item_in):
        key_acc, value_acc = carry_in
        query_blk, grad_blk, total_blk = item_in
        query_parts = []
        key_parts = []
        value_parts = []
        for start_head in range(0, heads_loc, head_step):
            part = slice(start_head, start_head + head_step)
            scores = (
                jnp.einsum(
                    "bhe,lhe->hbl",
                    query_blk[:, part],
                    keys_all[:, part],
                    preferred_element_type=jnp.float32,
                )
                * score_scale
                + bias_row
            )
            probs_full = jnp.exp(scores - total_blk[part][..., None])
            d_probs = jnp.einsum(
                "bhe,lhe->hbl",
                grad_blk[:, part],
                values_all[:, part],
                preferred_element_type=jnp.float32,
            )
            row_dot = jnp.sum(probs_full * d_probs, -1, keepdims=True)
            d_scores = (probs_full * (d_probs - row_dot)).astype(jnp.bfloat16)
            query_parts.append(
                jnp.einsum(
                    "hbl,lhe->bhe", d_scores, keys_all[:, part], preferred_element_type=jnp.float32
                )
                * score_scale
            )
            key_parts.append(
                jnp.einsum(
                    "hbl,bhe->lhe", d_scores, query_blk[:, part], preferred_element_type=jnp.float32
                )
                * score_scale
            )
            value_parts.append(
                jnp.einsum(
                    "hbl,bhe->lhe",
                    probs_full.astype(jnp.bfloat16),
                    grad_blk[:, part],
                    preferred_element_type=jnp.float32,
                )
            )
        key_acc = key_acc + jnp.concatenate(key_parts, 1)
        value_acc = value_acc + jnp.concatenate(value_parts, 1)
        return ((key_acc, value_acc), jnp.concatenate(query_parts, 1))

    empty = jnp.zeros((length, heads_loc, head_width), jnp.float32)
    (key_grad, value_grad), query_grad = lax.scan(
        one_block, (empty, empty), (query_blocks, grad_blocks, log_total)
    )
    return (query_grad.reshape(length, heads_loc, head_width), key_grad, value_grad)


def local(
    hidden_in,
    key_bias,
    w_qkv,
    bias_q,
    bias_v,
    w_out,
    bias_out,
    gain_attn,
    shift_attn,
    w_up,
    bias_up,
    w_down,
    bias_down,
    gain_ffn,
    shift_ffn,
    grad_out,
):
    groups = lax.axis_size("seq")
    params = (
        lax.all_gather(w_qkv, "dp", axis=0, tiled=True),
        lax.all_gather(bias_q, "dp", axis=0, tiled=True),
        lax.all_gather(bias_v, "dp", axis=0, tiled=True),
        lax.all_gather(w_out, "dp", axis=0, tiled=True),
        lax.all_gather(bias_out, "dp", axis=0, tiled=True),
        lax.all_gather(gain_attn, "dp", axis=0, tiled=True),
        lax.all_gather(shift_attn, "dp", axis=0, tiled=True),
        lax.all_gather(w_up, "dp", axis=0, tiled=True),
        lax.all_gather(bias_up, "dp", axis=0, tiled=True),
        lax.all_gather(w_down, "dp", axis=0, tiled=True),
        lax.all_gather(bias_down, "dp", axis=0, tiled=True),
        lax.all_gather(gain_ffn, "dp", axis=0, tiled=True),
        lax.all_gather(shift_ffn, "dp", axis=0, tiled=True),
    )
    full_bias_q = params[1].astype(jnp.float32)
    full_bias_v = params[2].astype(jnp.float32)
    full_bias_out = params[4].astype(jnp.float32)
    full_gain_attn = params[5].astype(jnp.float32)
    full_shift_attn = params[6].astype(jnp.float32)
    full_bias_up = params[8].astype(jnp.float32)
    full_bias_down = params[10].astype(jnp.float32)
    full_gain_ffn = params[11].astype(jnp.float32)
    full_shift_ffn = params[12].astype(jnp.float32)
    tok_rows, model_width = hidden_in.shape
    group_width = model_width // groups
    heads_loc = group_width // HEAD_DIM
    score_scale = HEAD_DIM ** (-0.5)
    no_bias = jnp.zeros((model_width,), jnp.float32)
    qkv_rows = matmul(hidden_in, params[0]) + jnp.concatenate([full_bias_q, no_bias, full_bias_v])
    qkv_rows = qkv_rows.astype(jnp.bfloat16).reshape(tok_rows, 3, groups, group_width)
    heads_in = lax.all_to_all(qkv_rows, "seq", split_axis=2, concat_axis=0, tiled=True)
    length = heads_in.shape[0]
    queries = heads_in[:, 0, 0].reshape(length, heads_loc, HEAD_DIM)
    keys_all = heads_in[:, 1, 0].reshape(length, heads_loc, HEAD_DIM)
    values_all = heads_in[:, 2, 0].reshape(length, heads_loc, HEAD_DIM)
    bias_row = lax.all_gather(key_bias, "seq", axis=1, tiled=True)[0]
    context_heads, log_total = attend_forward(queries, keys_all, values_all, bias_row, score_scale)
    context = lax.all_to_all(
        shortened(context_heads.reshape(length, 1, group_width)),
        "seq",
        split_axis=0,
        concat_axis=1,
        tiled=True,
    ).reshape(tok_rows, model_width)
    attended = hidden_in.astype(jnp.float32) + matmul(context, params[3]) + full_bias_out
    normed = layer_norm(attended, full_gain_attn, full_shift_attn)
    normed_low = normed.astype(jnp.bfloat16)
    pre_act = matmul(normed_low, params[7]) + full_bias_up
    activ = gelu_exact(pre_act).astype(jnp.bfloat16)
    branch_sum = normed + matmul(activ, params[9]) + full_bias_down
    output = layer_norm(branch_sum, full_gain_ffn, full_shift_ffn).astype(jnp.bfloat16)
    matrices = (
        lax.all_gather(w_qkv, "dp", axis=0, tiled=True),
        lax.all_gather(w_out, "dp", axis=0, tiled=True),
        lax.all_gather(w_up, "dp", axis=0, tiled=True),
        lax.all_gather(w_down, "dp", axis=0, tiled=True),
    )
    upstream = grad_out.astype(jnp.float32)
    _, norm_back = jax.vjp(layer_norm, branch_sum, full_gain_ffn, full_shift_ffn)
    d_branch, grad_gain_ffn, grad_shift_ffn = norm_back(upstream)
    grad_bias_down = jnp.sum(d_branch, 0)
    d_branch_low = d_branch.astype(jnp.bfloat16)
    grad_w_down = matmul_left(activ, d_branch_low)
    d_activ = matmul_right(d_branch_low, matrices[3])
    _, gelu_back = jax.vjp(gelu_exact, pre_act)
    d_pre = gelu_back(d_activ)[0]
    grad_bias_up = jnp.sum(d_pre, 0)
    d_pre_low = d_pre.astype(jnp.bfloat16)
    grad_w_up = matmul_left(normed_low, d_pre_low)
    d_normed = d_branch + matmul_right(d_pre_low, matrices[2])
    _, attn_norm_back = jax.vjp(layer_norm, attended, full_gain_attn, full_shift_attn)
    d_attended, grad_gain_attn, grad_shift_attn = attn_norm_back(d_normed)
    grad_bias_out = jnp.sum(d_attended, 0)
    d_attended_low = d_attended.astype(jnp.bfloat16)
    grad_w_out = matmul_left(context, d_attended_low)
    d_context = matmul_right(d_attended_low, matrices[1]).astype(jnp.bfloat16)
    d_context_heads = lax.all_to_all(
        d_context.reshape(tok_rows, groups, group_width),
        "seq",
        split_axis=1,
        concat_axis=0,
        tiled=True,
    )
    query_grad, key_grad, value_grad = attend_backward(
        queries,
        keys_all,
        values_all,
        bias_row,
        score_scale,
        log_total,
        d_context_heads.reshape(length, heads_loc, HEAD_DIM),
    )
    d_heads = (
        jnp.stack([query_grad, key_grad, value_grad], 1)
        .astype(jnp.bfloat16)
        .reshape(length, 3, 1, group_width)
    )
    d_qkv = lax.all_to_all(d_heads, "seq", split_axis=0, concat_axis=2, tiled=True).reshape(
        tok_rows, 3 * model_width
    )
    grad_bias_q = jnp.sum(d_qkv[:, :model_width].astype(jnp.float32), 0)
    grad_bias_v = jnp.sum(d_qkv[:, 2 * model_width :].astype(jnp.float32), 0)
    grad_w_qkv = matmul_left(hidden_in, d_qkv)
    grad_in = d_attended + matmul_right(d_qkv, matrices[0])
    local_grads = (
        grad_w_qkv,
        grad_bias_q,
        grad_bias_v,
        grad_w_out,
        grad_bias_out,
        grad_gain_attn,
        grad_shift_attn,
        grad_w_up,
        grad_bias_up,
        grad_w_down,
        grad_bias_down,
        grad_gain_ffn,
        grad_shift_ffn,
    )
    shares = (
        lax.psum_scatter(
            local_grads[0].astype(jnp.bfloat16), "dp", scatter_dimension=0, tiled=True
        ).astype(jnp.float32),
        lax.psum_scatter(
            local_grads[1].astype(jnp.bfloat16), "dp", scatter_dimension=0, tiled=True
        ).astype(jnp.float32),
        lax.psum_scatter(
            local_grads[2].astype(jnp.bfloat16), "dp", scatter_dimension=0, tiled=True
        ).astype(jnp.float32),
        lax.psum_scatter(
            local_grads[3].astype(jnp.bfloat16), "dp", scatter_dimension=0, tiled=True
        ).astype(jnp.float32),
        lax.psum_scatter(
            local_grads[4].astype(jnp.bfloat16), "dp", scatter_dimension=0, tiled=True
        ).astype(jnp.float32),
        lax.psum_scatter(
            local_grads[5].astype(jnp.bfloat16), "dp", scatter_dimension=0, tiled=True
        ).astype(jnp.float32),
        lax.psum_scatter(
            local_grads[6].astype(jnp.bfloat16), "dp", scatter_dimension=0, tiled=True
        ).astype(jnp.float32),
        lax.psum_scatter(
            local_grads[7].astype(jnp.bfloat16), "dp", scatter_dimension=0, tiled=True
        ).astype(jnp.float32),
        lax.psum_scatter(
            local_grads[8].astype(jnp.bfloat16), "dp", scatter_dimension=0, tiled=True
        ).astype(jnp.float32),
        lax.psum_scatter(
            local_grads[9].astype(jnp.bfloat16), "dp", scatter_dimension=0, tiled=True
        ).astype(jnp.float32),
        lax.psum_scatter(
            local_grads[10].astype(jnp.bfloat16), "dp", scatter_dimension=0, tiled=True
        ).astype(jnp.float32),
        lax.psum_scatter(
            local_grads[11].astype(jnp.bfloat16), "dp", scatter_dimension=0, tiled=True
        ).astype(jnp.float32),
        lax.psum_scatter(
            local_grads[12].astype(jnp.bfloat16), "dp", scatter_dimension=0, tiled=True
        ).astype(jnp.float32),
    )
    owned_grads = (
        lax.psum(shares[0].astype(jnp.bfloat16), "seq").astype(jnp.float32),
        lax.psum(shares[1].astype(jnp.bfloat16), "seq").astype(jnp.float32),
        lax.psum(shares[2].astype(jnp.bfloat16), "seq").astype(jnp.float32),
        lax.psum(shares[3].astype(jnp.bfloat16), "seq").astype(jnp.float32),
        lax.psum(shares[4].astype(jnp.bfloat16), "seq").astype(jnp.float32),
        lax.psum(shares[5].astype(jnp.bfloat16), "seq").astype(jnp.float32),
        lax.psum(shares[6].astype(jnp.bfloat16), "seq").astype(jnp.float32),
        lax.psum(shares[7].astype(jnp.bfloat16), "seq").astype(jnp.float32),
        lax.psum(shares[8].astype(jnp.bfloat16), "seq").astype(jnp.float32),
        lax.psum(shares[9].astype(jnp.bfloat16), "seq").astype(jnp.float32),
        lax.psum(shares[10].astype(jnp.bfloat16), "seq").astype(jnp.float32),
        lax.psum(shares[11].astype(jnp.bfloat16), "seq").astype(jnp.float32),
        lax.psum(shares[12].astype(jnp.bfloat16), "seq").astype(jnp.float32),
    )
    return (
        output,
        grad_in,
        owned_grads[0],
        owned_grads[1],
        owned_grads[2],
        owned_grads[3],
        owned_grads[4],
        owned_grads[5],
        owned_grads[6],
        owned_grads[7],
        owned_grads[8],
        owned_grads[9],
        owned_grads[10],
        owned_grads[11],
        owned_grads[12],
    )


def solution(mesh):
    return jax.shard_map(
        local,
        mesh=mesh,
        in_specs=(
            P(("dp", "seq"), None),
            P("dp", "seq"),
            P("dp", None),
            P("dp"),
            P("dp"),
            P("dp", None),
            P("dp"),
            P("dp"),
            P("dp"),
            P("dp", None),
            P("dp"),
            P("dp", None),
            P("dp"),
            P("dp"),
            P("dp"),
            P(("dp", "seq"), None),
        ),
        out_specs=(
            P(("dp", "seq"), None),
            P(("dp", "seq"), None),
            P("dp", None),
            P("dp"),
            P("dp"),
            P("dp", None),
            P("dp"),
            P("dp"),
            P("dp"),
            P("dp", None),
            P("dp"),
            P("dp", None),
            P("dp"),
            P("dp"),
            P("dp"),
        ),
        check_vma=False,
    )
```

profile of v0, /device:TPU:0, one launch (start us, length us, event | category | flops | bytes accessed | tf_op | source)
XLA Modules:
  0.0 1988.5 jit_solution(5152587531738367793)
XLA Ops:
  9.4 22.5 %all-gather.1 = bf16[8,1,128]{2,1,0:T(2,128)(2,1)S(1)} all-gather(bf16[1,1,128]{2,1,0:T(2,128)(2,1)} %bitcast.231), channel_id=1, replica_groups=mesh['dp'=8,'seq'=4] {'dp'}, dimensions={0}, use_global_device_ids=true | all-gather | bytes 2304 | tf_op jit(solution)/shard_map/all_gather | solution.py:174
  48.6 63.4 %all-gather.14.cloned.1.call-done = bf16[1024,3072]{1,0:T(8,128)(2,1)} async-done(((bf16[128,3072]{1,0:T(8,128)(2,1)}), bf16[1024,3072]{1,0:T(8,128)(2,1)}) %all-gather.14.cloned.1.call-update) | async-done | bytes 6291472 | tf_op jit(solution)/shard_map/all_gather | solution.py:172
  141.7 54.1 %all_gather.49 = f32[1,3072]{1,0:T(1,128)S(1)} all-gather(f32[1,768]{1,0:T(1,128)S(1)} %copy-done.34), channel_id=1, replica_groups=mesh['dp'=8,'seq'=4] {'seq'}, dimensions={1}, use_global_device_ids=true | all-gather | bytes 15360 | tf_op jit(solution)/shard_map/all_gather | solution.py:207
  213.4 180.6 %while.27 = (s32[]{:T(128)}, bf16[6,512,4,64]{1,3,2,0:T(8,128)(2,1)}, f32[6,4,512]{2,1,0:T(4,128)S(1)}, bf16[6,512,4,64]{1,3,2,0:T(8,128)(2,1)}, bf16[3072,4,64]...) while((s32[]{:T(128)}, bf16[6,512,4,64]{1,3,2,0:T(8,128)(2,1)}, ...), condition=%wide.region_5.6_spmd, body=%wide.region_0.5_spmd.sunk | while | flops 1686765568 | bytes 80098904 | solution.py:83
  399.7 22.8 %reshape.246 = bf16[3072,1,256]{2,1,0:T(2,128)(2,1)} reshape(bf16[6,512,4,64]{3,2,1,0:T(4,128)(2,1)} %copy.114) | data formatting | bytes 3145728 | tf_op jit(solution)/shard_map/reshape;reshape | solution.py:210
  445.9 17.5 all-gather.2
  480.2 17.5 all-gather.4
  497.7 26.0 %all-gather.5 = bf16[8,1,512]{2,1,0:T(2,128)(2,1)S(1)} all-gather(bf16[1,1,512]{2,1,0:T(2,128)(2,1)S(1)} %reshape.229), channel_id=1, replica_groups=mesh['dp'=8,'seq'=4] {'dp'}, dimensions={0}, use_global_device_ids=true | all-gather | bytes 9216 | tf_op jit(solution)/shard_map/all_gather | solution.py:180
  539.9 18.2 all-gather.7
  586.4 39.4 %multiply_convert_fusion.2 = (bf16[768,4096]{1,0:T(8,128)(2,1)}, f32[768,4096]{1,0:T(8,128)}, f32[768,4096]{1,0:T(8,128)}) fusion(f32[4096]{0:T(1024)S(1)} %bitcast.222, bf16[1024,4096]{1,0:T(8,128)(2,1)} %all-gather.18.cloned.1.call-done, f32[768,1024]{1,0:T(8,128)S(1)} %get-tuple-element.410, f32[1024]{0:T(1024)S(1)} %bitcast.226, ...), kind=kOutput, calls=%fused_computation.100 | convolution fusion | flops 6654001152 | bytes 43022336 | tf_op jit(solution)/shard_map/dot_general | solution.py:32
  642.8 21.7 %fusion.106 = (bf16[4096]{0:T(1024)(128)(2,1)}, bf16[768,4096]{1,0:T(8,128)(2,1)}) fusion(f32[768,4096]{1,0:T(8,128)} %get-tuple-element.392, bf16[4096,1024]{1,0:T(8,128)(2,1)} %all-gather.20.cloned.1.call-done, f32[768,1024]{1,0:T(8,128)} %get-tuple-element.390, f32[768]{0:T(1024)S(1)} %negate_multiply_fusion.2, f32[768,4096]{1,0:T(8,128)} %get-tuple-element.411, ...), kind=kOutput, calls=%fused_computation.167 | convolution fusion | flops 6494351360 | bytes 43019264 | tf_op jit(solution)/shard_map/dot_general | solution.py:42
  687.8 20.0 %all-to-all-done.2 = bf16[768,4,256]{0,2,1:T(8,128)(2,1)S(1)} async-done(((bf16[768,4,256]{0,2,1:T(8,128)(2,1)}), bf16[768,4,256]{0,2,1:T(8,128)(2,1)S(1)}, u32[]{:S(2)}, u32[]{:S(2)}) %all-to-all-start.2) | async-done | bytes 1572896 | tf_op jit(solution)/shard_map/all_to_all | solution.py:248
  717.6 568.6 %while.28 = (s32[]{:T(128)}, f32[3072,4,64]{0,2,1:T(8,128)}, f32[3072,4,64]{0,2,1:T(8,128)}, bf16[6,512,4,64]{1,3,2,0:T(8,128)(2,1)}, bf16[6,512,4,64]{1,3,2,0:T...) while((s32[]{:T(128)}, f32[3072,4,64]{0,2,1:T(8,128)}, ...), condition=%wide.region_17.18_spmd.clone, body=%wide.region_14.17_spmd.clone.sunk | while | flops 4127193088 | bytes 341160832 | solution.py:146
  740.8 20.1 %multiply_reduce_fusion.7 = (f32[2,512]{1,0:T(2,128)S(1)}, f32[2,512]{1,0:T(2,128)S(1)}, f32[2,512,3072]{2,1,0:T(8,128)}) fusion(f32[2,512,3072]{2,1,0:T(8,128)} %fusion.191, f32[2,512]{1,0:T(2,128)S(1)} %get-tuple-element.546, f32[3072]{0:T(1024)S(1)} %bitcast.204, f32[2,512,3072]{2,1,0:T(8,128)} %fusion.192, f32[2,512]{1,0:T(2,128)S(1)} %get-tuple-element.547, ...), kind=kOutput, calls=%fused_computation.39.clone.1 | convolution fusion | flops 434108416 | bytes 51409408 | tf_op jit(solution)/shard_map/while/body/eval_jaxpr/bhe,lhe->hbl/dot_general | solution.py:113
  760.9 17.9 multiply_convert_fusion.4
  834.0 20.1 %multiply_reduce_fusion.7 = (f32[2,512]{1,0:T(2,128)S(1)}, f32[2,512]{1,0:T(2,128)S(1)}, f32[2,512,3072]{2,1,0:T(8,128)}) fusion(f32[2,512,3072]{2,1,0:T(8,128)} %fusion.191, f32[2,512]{1,0:T(2,128)S(1)} %get-tuple-element.546, f32[3072]{0:T(1024)S(1)} %bitcast.204, f32[2,512,3072]{2,1,0:T(8,128)} %fusion.192, f32[2,512]{1,0:T(2,128)S(1)} %get-tuple-element.547, ...), kind=kOutput, calls=%fused_computation.39.clone.1 | convolution fusion | flops 434108416 | bytes 51409408 | tf_op jit(solution)/shard_map/while/body/eval_jaxpr/bhe,lhe->hbl/dot_general | solution.py:113
  854.0 17.9 multiply_convert_fusion.4
  928.9 20.0 %multiply_reduce_fusion.7 = (f32[2,512]{1,0:T(2,128)S(1)}, f32[2,512]{1,0:T(2,128)S(1)}, f32[2,512,3072]{2,1,0:T(8,128)}) fusion(f32[2,512,3072]{2,1,0:T(8,128)} %fusion.191, f32[2,512]{1,0:T(2,128)S(1)} %get-tuple-element.546, f32[3072]{0:T(1024)S(1)} %bitcast.204, f32[2,512,3072]{2,1,0:T(8,128)} %fusion.192, f32[2,512]{1,0:T(2,128)S(1)} %get-tuple-element.547, ...), kind=kOutput, calls=%fused_computation.39.clone.1 | convolution fusion | flops 434108416 | bytes 51409408 | tf_op jit(solution)/shard_map/while/body/eval_jaxpr/bhe,lhe->hbl/dot_general | solution.py:113
  948.9 17.9 multiply_convert_fusion.4
  1023.8 20.1 %multiply_reduce_fusion.7 = (f32[2,512]{1,0:T(2,128)S(1)}, f32[2,512]{1,0:T(2,128)S(1)}, f32[2,512,3072]{2,1,0:T(8,128)}) fusion(f32[2,512,3072]{2,1,0:T(8,128)} %fusion.191, f32[2,512]{1,0:T(2,128)S(1)} %get-tuple-element.546, f32[3072]{0:T(1024)S(1)} %bitcast.204, f32[2,512,3072]{2,1,0:T(8,128)} %fusion.192, f32[2,512]{1,0:T(2,128)S(1)} %get-tuple-element.547, ...), kind=kOutput, calls=%fused_computation.39.clone.1 | convolution fusion | flops 434108416 | bytes 51409408 | tf_op jit(solution)/shard_map/while/body/eval_jaxpr/bhe,lhe->hbl/dot_general | solution.py:113
  1043.9 17.9 multiply_convert_fusion.4
  1118.9 20.0 %multiply_reduce_fusion.7 = (f32[2,512]{1,0:T(2,128)S(1)}, f32[2,512]{1,0:T(2,128)S(1)}, f32[2,512,3072]{2,1,0:T(8,128)}) fusion(f32[2,512,3072]{2,1,0:T(8,128)} %fusion.191, f32[2,512]{1,0:T(2,128)S(1)} %get-tuple-element.546, f32[3072]{0:T(1024)S(1)} %bitcast.204, f32[2,512,3072]{2,1,0:T(8,128)} %fusion.192, f32[2,512]{1,0:T(2,128)S(1)} %get-tuple-element.547, ...), kind=kOutput, calls=%fused_computation.39.clone.1 | convolution fusion | flops 434108416 | bytes 51409408 | tf_op jit(solution)/shard_map/while/body/eval_jaxpr/bhe,lhe->hbl/dot_general | solution.py:113
  1138.9 17.9 multiply_convert_fusion.4
  1213.8 20.1 %multiply_reduce_fusion.7 = (f32[2,512]{1,0:T(2,128)S(1)}, f32[2,512]{1,0:T(2,128)S(1)}, f32[2,512,3072]{2,1,0:T(8,128)}) fusion(f32[2,512,3072]{2,1,0:T(8,128)} %fusion.191, f32[2,512]{1,0:T(2,128)S(1)} %get-tuple-element.546, f32[3072]{0:T(1024)S(1)} %bitcast.204, f32[2,512,3072]{2,1,0:T(8,128)} %fusion.192, f32[2,512]{1,0:T(2,128)S(1)} %get-tuple-element.547, ...), kind=kOutput, calls=%fused_computation.39.clone.1 | convolution fusion | flops 434108416 | bytes 51409408 | tf_op jit(solution)/shard_map/while/body/eval_jaxpr/bhe,lhe->hbl/dot_general | solution.py:113
  1233.9 17.9 multiply_convert_fusion.4
  1309.3 74.6 %all_to_all.63 = bf16[3072,3,1,256]{3,1,2,0:T(4,128)(2,1)S(1)} all-to-all(bf16[3072,3,1,256]{3,1,2,0:T(4,128)(2,1)} %copy.110), channel_id=1, replica_groups=mesh['dp'=8,'seq'=4] {'seq'}, dimensions={0} | all-to-all | bytes 9437184 | tf_op jit(solution)/shard_map/all_to_all | solution.py:269
  1453.9 36.6 %all-reduce.9 = (bf16[1024]{0:T(1024)(128)(2,1)S(1)}, bf16[1024]{0:T(1024)(128)(2,1)S(1)}, bf16[1024]{0:T(1024)(128)(2,1)S(1)}, bf16[1024]{0:T(1024)(128)(2,1)S(...) all-reduce(bf16[1024]{0:T(1024)(128)(2,1)S(1)} %get-tuple-element.3, ...), channel_id=3, replica_groups=mesh['dp'=8,'seq'=4] {'dp'}, use_global_device_ids=true, to_apply=%region_21.22.clone | all-reduce | flops 12288 | bytes 49152
  1501.6 26.6 %reduce-scatter.13.cloned.1.call-done = bf16[128,3072]{1,0:T(8,128)(2,1)} async-done(((bf16[1024,3072]{1,0:T(8,128)(2,1)}), bf16[128,3072]{1,0:T(8,128)(2,1)}) %reduce-scatter.13.cloned.1.call-update) | async-done | bytes 786448
  1530.4 68.5 %reduce-scatter.7.cloned.1.call-done = bf16[128,1024]{1,0:T(8,128)(2,1)} async-done(((bf16[1024,1024]{1,0:T(8,128)(2,1)}), bf16[128,1024]{1,0:T(8,128)(2,1)}) %reduce-scatter.7.cloned.1.call-update) | async-done | bytes 262160 | tf_op jit(solution)/shard_map/reduce_scatter | solution.py:301
  1598.9 151.6 %reduce-scatter.11.cloned.1.call-done = bf16[512,1024]{1,0:T(8,128)(2,1)} async-done(((bf16[4096,1024]{1,0:T(8,128)(2,1)}), bf16[512,1024]{1,0:T(8,128)(2,1)}) %reduce-scatter.11.cloned.1.call-update) | async-done | bytes 1048592 | tf_op jit(solution)/shard_map/reduce_scatter | solution.py:319
  1750.6 152.1 %reduce-scatter.9.cloned.1.call-done = bf16[128,4096]{1,0:T(8,128)(2,1)} async-done(((bf16[1024,4096]{1,0:T(8,128)(2,1)}), bf16[128,4096]{1,0:T(8,128)(2,1)}) %reduce-scatter.9.cloned.1.call-update) | async-done | bytes 1048592 | tf_op jit(solution)/shard_map/reduce_scatter | solution.py:313
  1912.6 61.3 %all-reduce.14.cloned.1.call-done = (bf16[128,3072]{0,1:T(8,128)(2,1)}, bf16[128,1024]{1,0:T(8,128)(2,1)}, bf16[128,4096]{1,0:T(8,128)(2,1)}, bf16[512,1024]{1,0:T(8,128)(2,1)}) async-done(((bf16[128,3072]{0,1:T(8,128)(2,1)}, bf16[128,1024]{1,0:T(8,128)(2,1)}, bf16[128,4096]{1,0:T(8,128)(2,1)}, bf16[512,1024]{1,0:T(8,128)(2,1)}), (bf16[128,3072]{0,1:T(8,128)(2,1)}, bf16[128,1024]{1,0:T(8,128)(2,1)}, ...) | async-done | bytes 3145744 | tf_op jit(solution)/shard_map/psum | solution.py:333
  (445 shorter events, 848.9 us)
Async XLA Ops:
  7.2 104.8 %all-gather.14.cloned.1.call-start = ((), (), s32[]{:S(2)}) async-start(), calls=%async_computation.8 | async-start | bytes 7077888 | tf_op jit(solution)/shard_map/all_gather | solution.py:172
  7.9 573.4 %all-gather.16.cloned.1.call-start = ((), (), s32[]{:S(2)}) async-start(), calls=%async_computation.9 | async-start | bytes 2359296 | tf_op jit(solution)/shard_map/all_gather | solution.py:175
  8.7 577.7 %all-gather.18.cloned.1.call-start = ((), (), s32[]{:S(2)}) async-start(), calls=%async_computation.10 | async-start | bytes 9437184 | tf_op jit(solution)/shard_map/all_gather | solution.py:179
  135.9 59.9 %all-to-all-start = ((bf16[768,3,4,256]{3,0,1,2:T(8,128)(2,1)}), bf16[768,3,4,256]{3,0,1,2:T(8,128)(2,1)}, u32[]{:S(2)}, u32[]{:S(2)}) async-start(bf16[768,3,4,256]{3,0,1,2:T(8,128)(2,1)} %copy.96), calls=%async_computation | async-start | bytes 9437184 | tf_op jit(solution)/shard_map/all_to_all | solution.py:202
  141.1 484.7 %all-gather.20.cloned.1.call-start = ((), (), s32[]{:S(2)}) async-start(), calls=%async_computation.11 | async-start | bytes 9437184 | tf_op jit(solution)/shard_map/all_gather | solution.py:181
  394.0 28.4 %copy-start.1 = (bf16[3072,4,64]{0,2,1:T(8,128)(2,1)}, bf16[3072,4,64]{0,2,1:T(8,128)(2,1)S(1)}, u32[]{:S(2)}) copy-start(bf16[3072,4,64]{0,2,1:T(8,128)(2,1)S(1)} %get-tuple-element.634) | copy-start | bytes 4718596
  394.0 28.4 %copy-start.14 = (f32[1,3072]{1,0:T(1,128)}, f32[1,3072]{1,0:T(1,128)S(1)}, u32[]{:S(2)}) copy-start(f32[1,3072]{1,0:T(1,128)S(1)} %get-tuple-element.653) | copy-start | bytes 36868
  394.0 28.4 %copy-start.21 = (f32[6,4,512]{2,1,0:T(4,128)}, f32[6,4,512]{2,1,0:T(4,128)S(1)}, u32[]{:S(2)}) copy-start(f32[6,4,512]{2,1,0:T(4,128)S(1)} %get-tuple-element.586) | copy-start | bytes 147460
  422.9 22.9 %copy-start.38 = (bf16[128]{0:T(256)(128)(2,1)S(1)}, bf16[128]{0:T(256)(128)(2,1)}, u32[]{:S(2)}) copy-start(bf16[128]{0:T(256)(128)(2,1)} %param.26) | copy-start | bytes 772
  422.9 40.4 %copy-start.39 = (bf16[128]{0:T(256)(128)(2,1)S(1)}, bf16[128]{0:T(256)(128)(2,1)}, u32[]{:S(2)}) copy-start(bf16[128]{0:T(256)(128)(2,1)} %param.27) | copy-start | bytes 772
  422.9 57.3 %copy-start.40 = (bf16[128]{0:T(256)(128)(2,1)S(1)}, bf16[128]{0:T(256)(128)(2,1)}, u32[]{:S(2)}) copy-start(bf16[128]{0:T(256)(128)(2,1)} %param.28) | copy-start | bytes 772
  422.9 74.8 %copy-start.37 = (bf16[512]{0:T(512)(128)(2,1)S(1)}, bf16[512]{0:T(512)(128)(2,1)}, u32[]{:S(2)}) copy-start(bf16[512]{0:T(512)(128)(2,1)} %param.30) | copy-start | bytes 3076
  422.9 100.8 %copy-start.41 = (bf16[128]{0:T(256)(128)(2,1)S(1)}, bf16[128]{0:T(256)(128)(2,1)}, u32[]{:S(2)}) copy-start(bf16[128]{0:T(256)(128)(2,1)} %param.32) | copy-start | bytes 772
  423.0 117.0 %copy-start.42 = (bf16[128]{0:T(256)(128)(2,1)S(1)}, bf16[128]{0:T(256)(128)(2,1)}, u32[]{:S(2)}) copy-start(bf16[128]{0:T(256)(128)(2,1)} %param.33) | copy-start | bytes 772
  423.0 135.1 %copy-start.43 = (bf16[128]{0:T(256)(128)(2,1)S(1)}, bf16[128]{0:T(256)(128)(2,1)}, u32[]{:S(2)}) copy-start(bf16[128]{0:T(256)(128)(2,1)} %param.34) | copy-start | bytes 772
  441.5 132.8 %all-to-all-start.1 = ((bf16[4,2,98304]{2,1,0:T(2,128)(2,1)}), bf16[4,2,98304]{2,1,0:T(2,128)(2,1)}, u32[]{:S(2)}, u32[]{:S(2)}) async-start(bf16[4,2,98304]{2,1,0:T(2,128)(2,1)} %reshape.259), calls=%async_computation.1 | async-start | bytes 3145728 | tf_op jit(solution)/shard_map/all_to_all | solution.py:209
  480.2 197.7 %copy-start.24 = (f32[8,1,128]{2,1,0:T(1,128)}, f32[8,1,128]{2,1,0:T(1,128)S(1)}, u32[]{:S(2)}) copy-start(f32[8,1,128]{2,1,0:T(1,128)S(1)} %convert_element_type.240) | copy-start | bytes 12292
  497.7 128.1 %copy-start.32 = (f32[8,1,128]{2,1,0:T(1,128)}, f32[8,1,128]{2,1,0:T(1,128)S(1)}, u32[]{:S(2)}) copy-start(f32[8,1,128]{2,1,0:T(1,128)S(1)} %convert_element_type.241) | copy-start | bytes 12292
  585.9 92.1 %copy-start.8 = (f32[768,1024]{1,0:T(8,128)}, f32[768,1024]{1,0:T(8,128)S(1)}, u32[]{:S(2)}) copy-start(f32[768,1024]{1,0:T(8,128)S(1)} %get-tuple-element.410) | copy-start | bytes 9437188
  585.9 92.1 %copy-start.19 = (f32[768]{0:T(1024)}, f32[768]{0:T(1024)S(1)}, u32[]{:S(2)}) copy-start(f32[768]{0:T(1024)S(1)} %broadcast_multiply_fusion.1) | copy-start | bytes 9220
  586.4 91.6 %copy-start.26 = (f32[768]{0:T(1024)}, f32[768]{0:T(1024)S(1)}, u32[]{:S(2)}) copy-start(f32[768]{0:T(1024)S(1)} %fusion.94) | copy-start | bytes 9220
  642.8 21.7 %copy-start.28 = (f32[768]{0:T(1024)}, f32[768]{0:T(1024)S(1)}, u32[]{:S(2)}) copy-start(f32[768]{0:T(1024)S(1)} %negate_multiply_fusion.2) | copy-start | bytes 9220
  684.1 23.6 %all-to-all-start.2 = ((bf16[768,4,256]{0,2,1:T(8,128)(2,1)}), bf16[768,4,256]{0,2,1:T(8,128)(2,1)S(1)}, u32[]{:S(2)}, u32[]{:S(2)}) async-start(bf16[768,4,256]{0,2,1:T(8,128)(2,1)} %bitcast.33), calls=%async_computation.2 | async-start | bytes 3145728 | tf_op jit(solution)/shard_map/all_to_all | solution.py:248
  687.7 840.5 %reduce-scatter.13.cloned.1.call-start = ((), (), s32[]{:S(2)}) async-start(), calls=%async_computation.15 | async-start | bytes 7077888
  871.9 15.6 slice-start.3
  966.8 15.6 slice-start.3
  1061.8 15.6 slice-start.3
  1411.6 187.3 %reduce-scatter.7.cloned.1.call-start = ((), (), s32[]{:S(2)}) async-start(), calls=%async_computation.12 | async-start | bytes 2359296 | tf_op jit(solution)/shard_map/reduce_scatter | solution.py:301
  1418.0 332.5 %reduce-scatter.11.cloned.1.call-start = ((), (), s32[]{:S(2)}) async-start(), calls=%async_computation.14 | async-start | bytes 9437184 | tf_op jit(solution)/shard_map/reduce_scatter | solution.py:319
  1430.6 472.1 %reduce-scatter.9.cloned.1.call-start = ((), (), s32[]{:S(2)}) async-start(), calls=%async_computation.13 | async-start | bytes 9437184 | tf_op jit(solution)/shard_map/reduce_scatter | solution.py:313
  1444.9 529.0 %all-reduce.14.cloned.1.call-start = ((), (), s32[]{:S(2)}) async-start(), calls=%async_computation.16 | async-start | bytes 6291456 | tf_op jit(solution)/shard_map/psum | solution.py:333
  1451.3 451.4 %copy-start.12 = (f32[768,1024]{1,0:T(8,128)S(1)}, f32[768,1024]{1,0:T(8,128)}, u32[]{:S(2)}) copy-start(f32[768,1024]{1,0:T(8,128)} %copy-done.10) | copy-start | bytes 9437188
  (73 other events, 488.5 us)
Sparse Core Ops, SparseCore 0:
  10.2 101.7 all-gather.13
  114.1 47.4 all-gather.15
  163.8 123.4 all-gather.17
  289.2 123.1 all-gather.19
  1411.7 116.4 reduce-scatter.12
  1532.1 66.7 reduce-scatter.6
  1602.5 147.9 reduce-scatter.10
  1754.6 148.0 reduce-scatter.8
  1905.9 67.9 all-reduce.13
where the time goes:
time: 2000 us; the launch traced here: 1990 us
  matrix products  711 us (36%)
  waiting for transfers between devices  546 us (27%)
  blocking collectives  339 us (17%)
  other arithmetic  225 us (11%)
  local copies, waits for them, and re-layouts  137 us (7%)
    dot_general x24, matrix products, one_block(): jnp.einsum('bhe,lhe->hbl', query_blk[:, part], keys_all[:, part], preferr...  181 us
    dot_general x12, matrix products, one_block(): jnp.einsum('bhe,lhe->hbl', grad_blk[:, part], values_all[:, part], prefer...  167 us
    reduce_scatter x1, waiting for transfers between devices, local(): lax.psum_scatter(local_grads[7].astype(jnp.bfloat16), 'dp', scatter_dimen...  152 us
    reduce_scatter x1, waiting for transfers between devices, local(): lax.psum_scatter(local_grads[9].astype(jnp.bfloat16), 'dp', scatter_dimen...  152 us
    convert_element_type x6, other arithmetic, one_block(): d_scores = (probs_full * (d_probs - row_dot)).astype(jnp.bfloat16)  107 us
    all_to_all x1, blocking collectives, local(): lax.all_to_all(d_heads, 'seq', split_axis=0, concat_axis=2, tiled=True)  74.6 us
    reduce_scatter x1, waiting for transfers between devices, local(): lax.psum_scatter(local_grads[3].astype(jnp.bfloat16), 'dp', scatter_dimen...  68.5 us
    dot_general x12, matrix products, one_block(): jnp.einsum('hbl,lhe->bhe', probs_low, values_all[:, part], preferred_elem...  66.6 us
  transfers between devices with their start and end apart: 12, of which 7 were waited for; matrix products, arithmetic and copies ran while one was open for 19% of the time, Pallas kernels for 0%

commit v1 on v0

v1 whole, which is shorter than its diff:
```python
import functools

import jax
import jax.numpy as jnp
from jax import lax
from jax.experimental import pallas as pl
from jax.experimental.pallas import tpu as pltpu
from jax.sharding import PartitionSpec as P

HEAD_DIM = 64
LANES = 128
SCALE = HEAD_DIM**-0.5
norm_eps = 1e-05
F32 = jnp.float32
LOW = jnp.bfloat16


def layer_norm(hidden, gain_vec, shift_vec):
    row_mean = jnp.mean(hidden, -1, keepdims=True)
    centered = hidden - row_mean
    row_var = jnp.mean(centered * centered, -1, keepdims=True)
    return centered * lax.rsqrt(row_var + norm_eps) * gain_vec + shift_vec


def gelu_exact(pre_act):
    return jax.nn.gelu(pre_act, approximate=False)


def matmul(left, right):
    return jnp.dot(left, right, preferred_element_type=F32)


def matmul_left(left, right):
    return lax.dot_general(left, right, (((0,), (0,)), ((), ())), preferred_element_type=F32)


def matmul_right(left, right):
    return lax.dot_general(left, right, (((1,), (1,)), ((), ())), preferred_element_type=F32)


def thirds(value):
    first = value.astype(LOW)
    rest = value - first.astype(F32)
    second = rest.astype(LOW)
    third = (rest - second.astype(F32)).astype(LOW)
    return first.astype(F32), second.astype(F32), third.astype(F32)


def head_mask(rows, head):
    lane = lax.broadcasted_iota(jnp.int32, (rows, LANES), 1)
    return (lane < HEAD_DIM) if head == 0 else (lane >= HEAD_DIM)


def fill_keys(k_ref, v_ref, bias_ref, ka_ref, va_ref):
    rows = k_ref.shape[0]
    lane = lax.broadcasted_iota(jnp.int32, (rows, LANES), 1)
    first, second, third = thirds(bias_ref[...])
    extra = jnp.where(
        lane == 0, first, jnp.where(lane == 1, second, jnp.where(lane == 2, third, 1.0))
    )
    ka_ref[:, :LANES] = k_ref[...]
    ka_ref[:, LANES:] = jnp.where(lane < 6, extra, 0.0).astype(LOW)
    va_ref[:, :LANES] = v_ref[...]
    va_ref[:, LANES:] = jnp.where(lane < 3, 1.0, 0.0).astype(LOW)


def forward_kernel(q_ref, k_ref, v_ref, bias_ref, o_ref, qx_ref, ka_ref, va_ref):
    @pl.when(pl.program_id(0) == 0)
    def _():
        fill_keys(k_ref, v_ref, bias_ref, ka_ref, va_ref)

    rows = q_ref.shape[0]
    lane = lax.broadcasted_iota(jnp.int32, (rows, LANES), 1)
    queries = q_ref[...].astype(F32) * SCALE
    ones = jnp.where(lane < 3, 1.0, 0.0)
    outs = []
    for head in range(2):
        masked = jnp.where(head_mask(rows, head), queries, 0.0)
        wide = jnp.concatenate([masked, ones], 1).astype(LOW)
        scores = matmul_right(wide, ka_ref[...])
        row_max = jnp.max(scores, -1, keepdims=True)
        expo = jnp.exp(scores - row_max).astype(LOW)
        both = matmul(expo, va_ref[...])
        total = both[:, LANES : LANES + 1]
        outs.append(both[:, :LANES] / total)
        first, second, third = thirds(row_max + jnp.log(total))
        qx_ref[head] = jnp.where(
            lane == 3, -first, jnp.where(lane == 4, -second, jnp.where(lane == 5, -third, ones))
        ).astype(LOW)
    o_ref[...] = jnp.where(head_mask(rows, 0), outs[0], outs[1]).astype(LOW)


def backward_kernel(
    q_ref, k_ref, v_ref, kt_ref, bias_ref, qx_ref, o_ref, do_ref,
    dq_ref, dk_ref, dv_ref, ka_ref, va_ref, dk_acc, dv_acc, *, chunk,
):
    step = pl.program_id(0)

    @pl.when(step == 0)
    def _():
        fill_keys(k_ref, v_ref, bias_ref, ka_ref, va_ref)
        dk_acc[...] = jnp.zeros_like(dk_acc)
        dv_acc[...] = jnp.zeros_like(dv_acc)

    rows = q_ref.shape[0]
    length = k_ref.shape[0]
    lane = lax.broadcasted_iota(jnp.int32, (rows, LANES), 1)
    queries = q_ref[...].astype(F32) * SCALE
    grads = do_ref[...].astype(F32)
    dots = grads * o_ref[...].astype(F32)
    q_wide, g_wide, q_mask, g_mask = [], [], [], []
    for head in range(2):
        mask = head_mask(rows, head)
        masked = jnp.where(mask, queries, 0.0).astype(LOW)
        g_masked = jnp.where(mask, grads, 0.0).astype(LOW)
        delta = jnp.sum(jnp.where(mask, dots, 0.0), -1, keepdims=True)
        first, second, third = thirds(delta)
        extra = jnp.where(
            lane == 0, -first, jnp.where(lane == 1, -second, jnp.where(lane == 2, -third, 0.0))
        ).astype(LOW)
        q_mask.append(masked)
        g_mask.append(g_masked)
        q_wide.append(jnp.concatenate([masked, qx_ref[head]], 1))
        g_wide.append(jnp.concatenate([g_masked, extra], 1))
    q_rows = jnp.concatenate(q_mask, 0)
    g_rows = jnp.concatenate(g_mask, 0)
    dq_t = [jnp.zeros((LANES, rows), F32) for _ in range(2)]
    for start in range(0, length, chunk):
        part = slice(start, start + chunk)
        p_list, ds_list = [], []
        for head in range(2):
            probs = jnp.exp(matmul_right(ka_ref[part, :], q_wide[head]))
            d_scores = (probs * matmul_right(va_ref[part, :], g_wide[head])).astype(LOW)
            p_list.append(probs.astype(LOW))
            ds_list.append(d_scores)
            dq_t[head] = dq_t[head] + matmul(kt_ref[:, part], d_scores)
        dv_acc[part, :] += matmul(jnp.concatenate(p_list, 1), g_rows)
        dk_acc[part, :] += matmul(jnp.concatenate(ds_list, 1), q_rows)
    row = lax.broadcasted_iota(jnp.int32, (LANES, rows), 0)
    both = jnp.where(row < HEAD_DIM, dq_t[0], dq_t[1]) * SCALE
    dq_ref[...] = both.T.astype(LOW)

    @pl.when(step == pl.num_programs(0) - 1)
    def _():
        dk_ref[...] = dk_acc[...].astype(LOW)
        dv_ref[...] = dv_acc[...].astype(LOW)


def cost(length, matmuls):
    return pl.CostEstimate(
        flops=2 * 2 * matmuls * length * length * 256,
        bytes_accessed=10 * length * LANES * 2,
        transcendentals=2 * length * length,
    )


def attend_forward(queries, keys, values, bias_wide):
    length = queries.shape[0]
    rows = 256
    tile = pl.BlockSpec((rows, LANES), lambda i: (i, 0))
    whole = pl.BlockSpec((length, LANES), lambda i: (0, 0))
    return pl.pallas_call(
        forward_kernel,
        grid=(length // rows,),
        in_specs=[tile, whole, whole, whole],
        out_specs=[tile, pl.BlockSpec((2, rows, LANES), lambda i: (0, i, 0))],
        out_shape=[
            jax.ShapeDtypeStruct((length, LANES), LOW),
            jax.ShapeDtypeStruct((2, length, LANES), LOW),
        ],
        scratch_shapes=[pltpu.VMEM((length, 2 * LANES), LOW)] * 2,
        compiler_params=pltpu.CompilerParams(vmem_limit_bytes=48 * 2**20),
        cost_estimate=cost(length, 2),
    )(queries, keys, values, bias_wide)


def attend_backward(queries, keys, values, bias_wide, q_extra, context, context_grad):
    length = queries.shape[0]
    rows = 256
    chunk = 768 if length % 768 == 0 else 256
    tile = pl.BlockSpec((rows, LANES), lambda i: (i, 0))
    whole = pl.BlockSpec((length, LANES), lambda i: (0, 0))
    return pl.pallas_call(
        functools.partial(backward_kernel, chunk=chunk),
        grid=(length // rows,),
        in_specs=[
            tile, whole, whole, pl.BlockSpec((LANES, length), lambda i: (0, 0)), whole,
            pl.BlockSpec((2, rows, LANES), lambda i: (0, i, 0)), tile, tile,
        ],
        out_specs=[tile, whole, whole],
        out_shape=[jax.ShapeDtypeStruct((length, LANES), LOW)] * 3,
        scratch_shapes=[pltpu.VMEM((length, 2 * LANES), LOW)] * 2
        + [pltpu.VMEM((length, LANES), F32)] * 2,
        compiler_params=pltpu.CompilerParams(vmem_limit_bytes=48 * 2**20),
        cost_estimate=cost(length, 5),
    )(queries, keys, values, keys.T, bias_wide, q_extra, context, context_grad)


def swap(array, name, mask):
    return lax.ppermute(array, name, [(i, i ^ mask) for i in range(lax.axis_size(name))])


def bits(name):
    return lax.axis_size(name).bit_length() - 1


def bit_order(last):
    dp_bits = [("dp", k) for k in reversed(range(bits("dp")))]
    seq_bits = [("seq", k) for k in reversed(range(1, bits("seq")))]
    order = dp_bits + seq_bits
    if last in order:
        order.remove(last)
        order.append(last)
    return order + [("seq", 0)]


def place(name, k):
    return bits("dp") - 1 - k if name == "dp" else bits("dp") + bits("seq") - 1 - k


def my_bit(name, k):
    return (lax.axis_index(name) >> k) & 1


def double(array, name, k):
    other = swap(array, name, 1 << k)
    at = place(name, k)
    return jnp.where(
        my_bit(name, k) == 0,
        jnp.concatenate([array, other], at),
        jnp.concatenate([other, array], at),
    )


def gather_weight(shard, last):
    rows = shard.shape[0] // lax.axis_size("seq")
    own = lax.dynamic_slice_in_dim(shard, lax.axis_index("seq") * rows, rows, 0)
    own = own.reshape((1,) * (bits("dp") + bits("seq")) + own.shape)
    for name, k in bit_order(last):
        own = double(own, name, k)
    return own.reshape(-1, shard.shape[1])


def reduce_weight(grad, last):
    count = bits("dp") + bits("seq")
    rows = grad.shape[0] >> count
    part = grad.astype(LOW).reshape((2,) * count + (rows, grad.shape[1]))
    for name, k in reversed(bit_order(last)):
        mine = my_bit(name, k)
        away = lax.dynamic_index_in_dim(part, 1 - mine, place(name, k))
        keep = lax.dynamic_index_in_dim(part, mine, place(name, k))
        part = (keep.astype(F32) + swap(away, name, 1 << k).astype(F32)).astype(LOW)
    for k in reversed(range(bits("seq"))):
        part = double(part, "seq", k)
    return part.reshape(-1, grad.shape[1]).astype(F32)


def exchange(blocks):
    return [block if t == 0 else swap(block, "seq", t) for t, block in enumerate(blocks)]


def by_index(blocks):
    count = len(blocks)
    me = lax.axis_index("seq")
    return [lax.select_n(me, *[blocks[i ^ j] for i in range(count)]) for j in range(count)]


def columns(array, group, pair, group_width):
    return lax.dynamic_slice_in_dim(array, group * group_width + pair * LANES, LANES, 1)


def local(
    hidden_in, key_bias, w_qkv, bias_q, bias_v, w_out, bias_out, gain_attn, shift_attn,
    w_up, bias_up, w_down, bias_down, gain_ffn, shift_ffn, grad_out,
):
    groups = lax.axis_size("seq")
    me = lax.axis_index("seq")
    tok_rows, width = hidden_in.shape
    group_width = width // groups
    pairs = group_width // LANES
    wide_y, wide_x, wide_z = ("seq", 1), ("dp", 0), ("dp", 1)

    w_q = gather_weight(w_qkv[:, :width], wide_y)
    w_k = gather_weight(w_qkv[:, width : 2 * width], wide_x)
    w_v = gather_weight(w_qkv[:, 2 * width :], wide_z)
    vectors = (
        bias_q, bias_v, bias_out, gain_attn, shift_attn, bias_down, gain_ffn, shift_ffn, bias_up,
    )
    packed = lax.all_gather(jnp.concatenate(vectors), "dp", axis=0).astype(F32)
    fulls, at = [], 0
    for vector in vectors:
        fulls.append(packed[:, at : at + vector.shape[0]].reshape(-1))
        at += vector.shape[0]
    (f_bias_q, f_bias_v, f_bias_out, f_gain_attn, f_shift_attn, f_bias_down, f_gain_ffn,
     f_shift_ffn, f_bias_up) = fulls
    f_w_out = gather_weight(w_out, wide_z)
    f_w_up = gather_weight(w_up, wide_y)
    f_w_down = gather_weight(w_down, wide_x)

    q_rows = (matmul(hidden_in, w_q) + f_bias_q).astype(LOW)
    k_rows = matmul(hidden_in, w_k).astype(LOW)
    v_rows = (matmul(hidden_in, w_v) + f_bias_v).astype(LOW)
    bias_col = jnp.concatenate(exchange([key_bias[0]] * groups))
    bias_wide = jnp.broadcast_to(bias_col[:, None], (bias_col.shape[0], LANES))
    saved, context_parts = [], []
    for pair in range(pairs):
        got = exchange([
            jnp.concatenate(
                [columns(rows, me ^ t, pair, group_width) for rows in (q_rows, k_rows, v_rows)], 1
            )
            for t in range(groups)
        ])
        queries, keys, values = (
            jnp.concatenate([block[:, i * LANES : (i + 1) * LANES] for block in got])
            for i in range(3)
        )
        context, q_extra = attend_forward(queries, keys, values, bias_wide)
        saved.append((queries, keys, values, bias_wide, q_extra, context))
        context_parts.append(by_index(exchange(
            [context[t * tok_rows : (t + 1) * tok_rows] for t in range(groups)]
        )))
    context = jnp.concatenate(
        [context_parts[pair][j] for j in range(groups) for pair in range(pairs)], 1
    )

    attended = hidden_in.astype(F32) + matmul(context, f_w_out) + f_bias_out
    normed = layer_norm(attended, f_gain_attn, f_shift_attn)
    normed_low = normed.astype(LOW)
    pre_act = matmul(normed_low, f_w_up) + f_bias_up
    activ = gelu_exact(pre_act).astype(LOW)
    branch_sum = normed + matmul(activ, f_w_down) + f_bias_down
    output = layer_norm(branch_sum, f_gain_ffn, f_shift_ffn).astype(LOW)

    upstream = grad_out.astype(F32)
    _, norm_back = jax.vjp(layer_norm, branch_sum, f_gain_ffn, f_shift_ffn)
    d_branch, g_gain_ffn, g_shift_ffn = norm_back(upstream)
    g_bias_down = jnp.sum(d_branch, 0)
    d_branch_low = d_branch.astype(LOW)
    g_w_down = matmul_left(activ, d_branch_low).astype(LOW)
    d_activ = matmul_right(d_branch_low, f_w_down)
    _, gelu_back = jax.vjp(gelu_exact, pre_act)
    d_pre = gelu_back(d_activ)[0]
    g_bias_up = jnp.sum(d_pre, 0)
    d_pre_low = d_pre.astype(LOW)
    g_w_up = matmul_left(normed_low, d_pre_low).astype(LOW)
    d_normed = d_branch + matmul_right(d_pre_low, f_w_up)
    _, attn_norm_back = jax.vjp(layer_norm, attended, f_gain_attn, f_shift_attn)
    d_attended, g_gain_attn, g_shift_attn = attn_norm_back(d_normed)
    g_bias_out = jnp.sum(d_attended, 0)
    d_attended_low = d_attended.astype(LOW)
    g_w_out = matmul_left(context, d_attended_low).astype(LOW)
    d_context = matmul_right(d_attended_low, f_w_out).astype(LOW)
    d_context, g_w_down, g_w_up, g_w_out = lax.optimization_barrier(
        (d_context, g_w_down, g_w_up, g_w_out)
    )
    s_w_down = reduce_weight(g_w_down, wide_x)
    s_w_up = reduce_weight(g_w_up, wide_y)
    s_w_out = reduce_weight(g_w_out, wide_z)

    grad_parts = []
    for pair in range(pairs):
        got = jnp.concatenate(exchange(
            [columns(d_context, me ^ t, pair, group_width) for t in range(groups)]
        ))
        d_heads = jnp.concatenate(attend_backward(*saved[pair], got), 1)
        grad_parts.append(by_index(exchange(
            [d_heads[t * tok_rows : (t + 1) * tok_rows] for t in range(groups)]
        )))
    d_q, d_k, d_v = (
        jnp.concatenate(
            [
                grad_parts[pair][j][:, i * LANES : (i + 1) * LANES]
                for j in range(groups)
                for pair in range(pairs)
            ],
            1,
        )
        for i in range(3)
    )
    s_w_q = reduce_weight(matmul_left(hidden_in, d_q), wide_y)
    s_w_k = reduce_weight(matmul_left(hidden_in, d_k), wide_x)
    s_w_v = reduce_weight(matmul_left(hidden_in, d_v), wide_z)
    g_bias_q = jnp.sum(d_q.astype(F32), 0)
    g_bias_v = jnp.sum(d_v.astype(F32), 0)
    grad_in = d_attended + matmul_right(d_q, w_q) + matmul_right(d_k, w_k) + matmul_right(d_v, w_v)

    vector_grads = (
        g_bias_q, g_bias_v, g_bias_out, g_gain_attn, g_shift_attn, g_bias_down, g_gain_ffn,
        g_shift_ffn, g_bias_up,
    )
    shares = lax.axis_size("dp")
    rows = jnp.concatenate([g.reshape(shares, -1) for g in vector_grads], 1).astype(LOW)
    own = lax.dynamic_index_in_dim(
        lax.psum(rows, ("dp", "seq")), lax.axis_index("dp"), 0, False
    ).astype(F32)
    sums, at = [], 0
    for vector in vectors:
        sums.append(own[at : at + vector.shape[0]])
        at += vector.shape[0]
    (s_bias_q, s_bias_v, s_bias_out, s_gain_attn, s_shift_attn, s_bias_down, s_gain_ffn,
     s_shift_ffn, s_bias_up) = sums
    return (
        output, grad_in, jnp.concatenate([s_w_q, s_w_k, s_w_v], 1), s_bias_q, s_bias_v, s_w_out,
        s_bias_out, s_gain_attn, s_shift_attn, s_w_up, s_bias_up, s_w_down, s_bias_down,
        s_gain_ffn, s_shift_ffn,
    )


def solution(mesh):
    tokens = P(("dp", "seq"), None)
    matrix = P("dp", None)
    vector = P("dp")
    return jax.shard_map(
        local,
        mesh=mesh,
        in_specs=(
            tokens, P("dp", "seq"), matrix, vector, vector, matrix, vector, vector, vector,
            matrix, vector, matrix, vector, vector, vector, tokens,
        ),
        out_specs=(
            tokens, tokens, matrix, vector, vector, matrix, vector, vector, vector, matrix,
            vector, matrix, vector, vector, vector,
        ),
        check_vma=False,
    )
```

time: 2000 us -> 959 us (0.48)
  matrix products: 711 us -> 139 us
  blocking collectives: 339 us -> 72 us
  waiting for transfers between devices: 546 us -> 309 us
  Pallas kernels: 0 us -> 195 us
  other arithmetic: 225 us -> 82.5 us
  starting transfers between devices: 13.4 us -> 94.3 us
  local copies, waits for them, and re-layouts: 137 us -> 59.9 us
    dot_general x88 -> x6, matrix products: 625 us -> 52 us  [matmul(): return jnp.dot(left, right, preferred_element_type=F32)]
    reduce_scatter x3 -> x0, waiting for transfers between devices: 372 us -> none  [the longest x1 152 us: local(): lax.psum_scatter(local_grads[7].astype(jnp.bfloat16), 'dp', scatter_dimen...]
    ppermute x0 -> x99, waiting for transfers between devices: none -> 309 us  [swap(): lax.ppermute(array, name, [(i, i ^ mask) for i in range(lax.axis_size(nam...]
    pallas_call x0 -> x4, Pallas kernels: none -> 195 us  [the longest x2 118 us: attend_backward(): pl.pallas_call(functools.partial(backward_kernel, chunk=chunk), grid=(len...]
    all_gather x10 -> x1, blocking collectives: 222 us -> 34.3 us  [local(): packed = lax.all_gather(jnp.concatenate(vectors), 'dp', axis=0).astype(F32)]
    convert_element_type x27 -> x34, other arithmetic: 119 us -> 22.2 us  [the longest x30 18.1 us: reduce_weight(): part = (keep.astype(F32) + swap(away, name, 1 << k).astype(F32)).astype(LOW)]
    ppermute x0 -> x99, starting transfers between devices: none -> 94.3 us  [swap(): lax.ppermute(array, name, [(i, i ^ mask) for i in range(lax.axis_size(nam...]
    all_to_all x1 -> x0, blocking collectives: 74.6 us -> none  [local(): lax.all_to_all(d_heads, 'seq', split_axis=0, concat_axis=2, tiled=True)]
  transfers between devices with their start and end apart: 12 -> 99, of which waited for: 7 -> 44; matrix products, arithmetic and copies ran while one was open for 19% -> 20% of each run, Pallas kernels for 0% -> 20%
where the time goes in v1:
time: 959 us; the launch traced here: 955 us
  waiting for transfers between devices  309 us (32%)
  Pallas kernels  195 us (20%)
  matrix products  139 us (14%)
  starting transfers between devices  94.3 us (10%)
  other arithmetic  82.5 us (9%)
  blocking collectives  72 us (8%)
  local copies, waits for them, and re-layouts  59.9 us (6%)
    ppermute x99, waiting for transfers between devices, swap(): lax.ppermute(array, name, [(i, i ^ mask) for i in range(lax.axis_size(nam...  309 us
    pallas_call x2, Pallas kernels, attend_backward(): pl.pallas_call(functools.partial(backward_kernel, chunk=chunk), grid=(len...  118 us
    ppermute x99, starting transfers between devices, swap(): lax.ppermute(array, name, [(i, i ^ mask) for i in range(lax.axis_size(nam...  94.3 us
    pallas_call x2, Pallas kernels, attend_forward(): pl.pallas_call(forward_kernel, grid=(length // rows,), in_specs=[tile, wh...  77.4 us
    dot_general x6, matrix products, matmul_right(): lax.dot_general(left, right, (((1,), (1,)), ((), ())), preferred_element_...  52.8 us
    dot_general x6, matrix products, matmul(): return jnp.dot(left, right, preferred_element_type=F32)  52 us
    psum x1, blocking collectives, local(): lax.psum(rows, ('dp', 'seq'))  37.7 us
    dot_general x6, matrix products, matmul_left(): lax.dot_general(left, right, (((0,), (0,)), ((), ())), preferred_element_...  34.6 us
  transfers between devices with their start and end apart: 99, of which 44 were waited for; matrix products, arithmetic and copies ran while one was open for 20% of the time, Pallas kernels for 20%

profile of v1, /device:TPU:0, one launch (start us, length us, event | category | flops | bytes accessed | tf_op | source)
XLA Modules:
  0.0 954.8 jit_solution(752871846108042945)
XLA Ops:
  11.8 34.3 %all-gather.1 = bf16[8,1,1536]{2,1,0:T(2,128)(2,1)S(1)} all-gather(bf16[1,1,1536]{2,1,0:T(2,128)(2,1)S(1)} %reshape.5114), channel_id=2, replica_groups=mesh['dp'=8,'seq'=4] {'dp'}, dimensions={0}, use_global_device_ids=true | all-gather | bytes 27648 | tf_op jit(solution)/shard_map/all_gather | solution.py:289
  91.5 8.7 collective-permute-done.41
  100.7 8.7 collective-permute-done.13
  117.4 10.6 %collective-permute-done.42 = bf16[2,2,1,1,1,128,1024]{6,5,4,3,2,1,0:T(8,128)(2,1)S(1)} collective-permute-done((bf16[2,2,1,1,1,128,1024]{6,5,4,3,2,1,0:T(8,128)(2,1)S(1)}, bf16[2,2,1,1,1,128,1024]{6,5,4,3,2,1,0:T(8,128)(2,1)S(1)}, u32[]{:S(2)}, u32[]{:S(2)}) %collective-permute-start.42) | collective-permute-done | bytes 1048608 | tf_op jit(solution)/shard_map/ppermute | solution.py:200
  152.1 34.6 %collective-permute-done.17 = bf16[768,384]{0,1:T(8,128)(2,1)S(1)} collective-permute-done((bf16[768,384]{0,1:T(8,128)(2,1)S(1)}, bf16[768,384]{0,1:T(8,128)(2,1)S(1)}, u32[]{:S(2)}, u32[]{:S(2)}) %collective-permute-start.17) | collective-permute-done | bytes 589856 | tf_op jit(solution)/shard_map/ppermute | solution.py:200
  188.7 10.0 %collective-permute-done.16 = bf16[768,384]{0,1:T(8,128)(2,1)S(1)} collective-permute-done((bf16[768,384]{0,1:T(8,128)(2,1)S(1)}, bf16[768,384]{0,1:T(8,128)(2,1)S(1)}, u32[]{:S(2)}, u32[]{:S(2)}) %collective-permute-start.16) | collective-permute-done | bytes 589856 | tf_op jit(solution)/shard_map/ppermute | solution.py:200
  207.5 38.6 %shard_map.271 = (bf16[3072,128]{1,0:T(8,128)(2,1)S(1)}, bf16[2,3072,128]{2,1,0:T(8,128)(2,1)S(1)}) custom-call(bf16[3072,128]{1,0:T(8,128)(2,1)S(1)} %copy.193.q_ref, bf16[3072,128]{1,0:T(8,128)(2,1)S(1)} %copy.194.k_ref, bf16[3072,128]{1,0:T(8,128)(2,1)S(1)} %copy.195.v_ref, f32[3072,128]{1,0:T(8,128)} %broadcast_in_dim.10.bias_ref), custom_call_target="tpu_custom_call" | custom-call | flops 19327352832 | bytes 7864320 | tf_op jit(solution)/shard_map/pallas_call | solution.py:162
  272.0 38.8 %shard_map.272 = (bf16[3072,128]{1,0:T(8,128)(2,1)S(1)}, bf16[2,3072,128]{2,1,0:T(8,128)(2,1)S(1)}) custom-call(bf16[3072,128]{1,0:T(8,128)(2,1)S(1)} %copy-done.2, bf16[3072,128]{1,0:T(8,128)(2,1)S(1)} %copy-done.4, bf16[3072,128]{1,0:T(8,128)(2,1)S(1)} %copy-done.6, f32[3072,128]{1,0:T(8,128)} %broadcast_in_dim.10.bias_ref), custom_call_target="tpu_custom_call" | custom-call | flops 19327352832 | bytes 7864320 | tf_op jit(solution)/shard_map/pallas_call | solution.py:162
  313.3 5.5 collective-permute-done.28
  332.7 5.3 maximum_select_fusion
  338.0 37.0 %multiply_convert_fusion = (bf16[768,4096]{1,0:T(8,128)(2,1)S(1)}, f32[768,4096]{1,0:T(8,128)}, f32[768,4096]{1,0:T(8,128)}) fusion(f32[4096]{0:T(1024)S(1)} %bitcast.358, bf16[1024,4096]{1,0:T(8,128)(2,1)S(1)} %bitcast.306, f32[768,1024]{1,0:T(8,128)S(1)} %get-tuple-element.211, f32[1024]{0:T(1024)S(1)} %copy-done.47, f32[1024]{0:T(1024)S(1)} %get-tuple-element.198, ...), kind=kOutput, calls=%fused_computation.3 | convolution fusion | flops 6654001152 | bytes 43022336 | tf_op jit(solution)/shard_map/dot_general | solution.py:30
  375.0 5.3 maximum_select_fusion.1
  380.3 7.1 fusion.73
  393.0 9.3 convolution_convert_fusion.1
  402.4 22.0 %fusion.74 = (bf16[4096]{0:T(1024)(128)(2,1)}, bf16[768,4096]{1,0:T(8,128)(2,1)}) fusion(f32[768,4096]{1,0:T(8,128)} %get-tuple-element.53, bf16[4096,1024]{1,0:T(8,128)(2,1)} %bitcast.309, f32[768,1024]{1,0:T(8,128)} %copy-done.18, f32[768]{0:T(1024)S(1)} %negate_multiply_fusion.2, f32[768,4096]{1,0:T(8,128)} %get-tuple-element.212, f32[4096]{0:T(1024)S(1)} %bitcast.359), kind=kOutput, calls=%fused_computation.383 | convolution fusion | flops 6494351360 | bytes 43019264 | tf_op jit(solution)/shard_map/dot_general | solution.py:38
  424.4 14.3 %multiply_reduce_fusion = (bf16[1024]{0:T(1024)(128)(2,1)}, f32[768]{0:T(1024)S(1)}, bf16[1024]{0:T(1024)(128)(2,1)}, f32[768,1024]{1,0:T(8,128)S(1)}) fusion(f32[768,1024]{1,0:T(8,128)} %copy-done.14, f32[768]{0:T(1024)S(1)} %fusion.44, f32[768]{0:T(1024)S(1)} %broadcast_multiply_fusion.1, f32[1024]{0:T(1024)S(1)} %get-tuple-element.198, ...), kind=kOutput, calls=%fused_computation.35 | convolution fusion | flops 6450312192 | bytes 24137728 | tf_op jit(solution)/shard_map/dot_general | solution.py:38
  438.7 12.3 %convolution_convert_fusion = bf16[1024,4096]{1,0:T(8,128)(2,1)} fusion(bf16[768,4096]{1,0:T(8,128)(2,1)} %get-tuple-element.217, f32[768,1024]{1,0:T(8,128)S(1)} %copy-done.15, f32[1024]{0:T(1024)S(1)} %copy-done.47, f32[1024]{0:T(1024)S(1)} %get-tuple-element.198, f32[768]{0:T(1024)S(1)} %fusion.44, f32[768]{0:T(1024)S(1)} %broadcast_multiply_fusion.1), kind=kOutput, calls=%fused_computation.21 | convolution fusion | flops 6450577408 | bytes 17840128 | tf_op jit(solution)/shard_map/dot_general | solution.py:34
  480.7 58.5 %shard_map.273 = (bf16[3072,128]{1,0:T(8,128)(2,1)S(1)}, bf16[3072,128]{1,0:T(8,128)(2,1)S(1)}, bf16[3072,128]{1,0:T(8,128)(2,1)S(1)}) custom-call(bf16[3072,128]{1,0:T(8,128)(2,1)S(1)} %copy.193.q_ref, bf16[3072,128]{1,0:T(8,128)(2,1)S(1)} %copy.194.k_ref, bf16[3072,128]{1,0:T(8,128)(2,1)S(1)} %copy.195.v_ref, bf16[128,3072]{1,0:T(8,128)(2,1)S(1)} %copy-done.8, ...), custom_call_target="tpu_custom_call" | custom-call | flops 48318382080 | bytes 7864320 | tf_op jit(solution)/shard_map/pallas_call | solution.py:183
  544.1 59.1 %shard_map.274 = (bf16[3072,128]{1,0:T(8,128)(2,1)S(1)}, bf16[3072,128]{1,0:T(8,128)(2,1)S(1)}, bf16[3072,128]{1,0:T(8,128)(2,1)S(1)}) custom-call(bf16[3072,128]{1,0:T(8,128)(2,1)S(1)} %copy-done.3, bf16[3072,128]{1,0:T(8,128)(2,1)S(1)} %copy-done.5, bf16[3072,128]{1,0:T(8,128)(2,1)S(1)} %copy-done.7, bf16[128,3072]{1,0:T(8,128)(2,1)S(1)} %copy-done.9, ...), custom_call_target="tpu_custom_call" | custom-call | flops 48318382080 | bytes 7864320 | tf_op jit(solution)/shard_map/pallas_call | solution.py:183
  606.8 12.5 %collective-permute-done.56 = bf16[768,384]{1,0:T(8,128)(2,1)S(1)} collective-permute-done((bf16[768,384]{1,0:T(8,128)(2,1)S(1)}, bf16[768,384]{1,0:T(8,128)(2,1)S(1)}, u32[]{:S(2)}, u32[]{:S(2)}) %collective-permute-start.56) | collective-permute-done | bytes 589856 | tf_op jit(solution)/shard_map/ppermute | solution.py:200
  619.4 13.1 %collective-permute-done.55 = bf16[768,384]{1,0:T(8,128)(2,1)S(1)} collective-permute-done((bf16[768,384]{1,0:T(8,128)(2,1)S(1)}, bf16[768,384]{1,0:T(8,128)(2,1)S(1)}, u32[]{:S(2)}, u32[]{:S(2)}) %collective-permute-start.55) | collective-permute-done | bytes 589856 | tf_op jit(solution)/shard_map/ppermute | solution.py:200
  656.0 37.7 %psum.7 = bf16[8,1536]{1,0:T(8,128)(2,1)S(1)} all-reduce(bf16[8,1536]{1,0:T(8,128)(2,1)S(1)} %constant_dynamic-update-slice_fusion.6), channel_id=1, replica_groups=mesh['dp'=8,'seq'=4] {'dp','seq'}, use_global_device_ids=true, to_apply=%region_17.18 | all-reduce | flops 12288 | bytes 49152 | tf_op jit(solution)/shard_map/psum | solution.py:394
  693.7 7.6 add_add_fusion.2
  707.7 9.3 collective-permute-done.79
  734.3 9.6 %collective-permute-done.82 = bf16[1,1,1,1,1,32,1024]{6,5,4,3,2,1,0:T(8,128)(2,1)S(1)} collective-permute-done((bf16[1,1,1,1,1,32,1024]{6,5,4,3,2,1,0:T(8,128)(2,1)S(1)}, bf16[1,1,1,1,1,32,1024]{6,5,4,3,2,1,0:T(8,128)(2,1)S(1)}, u32[]{:S(2)}, u32[]{:S(2)}) %collective-permute-start.82) | collective-permute-done | bytes 65568 | tf_op jit(solution)/shard_map/ppermute | solution.py:200
  754.3 5.5 collective-permute-done.65
  799.5 29.5 %collective-permute-done.86 = bf16[2,2,2,1,1,32,4096]{6,5,4,3,2,1,0:T(8,128)(2,1)S(1)} collective-permute-done((bf16[2,2,2,1,1,32,4096]{6,5,4,3,2,1,0:T(8,128)(2,1)S(1)}, bf16[2,2,2,1,1,32,4096]{6,5,4,3,2,1,0:T(8,128)(2,1)S(1)}, u32[]{:S(2)}, u32[]{:S(2)}) %collective-permute-start.86) | collective-permute-done | bytes 2097184 | tf_op jit(solution)/shard_map/ppermute | solution.py:200
  838.6 17.6 %collective-permute-done.87 = bf16[2,2,1,1,1,32,4096]{6,5,4,3,2,1,0:T(8,128)(2,1)S(1)} collective-permute-done((bf16[2,2,1,1,1,32,4096]{6,5,4,3,2,1,0:T(8,128)(2,1)S(1)}, bf16[2,2,1,1,1,32,4096]{6,5,4,3,2,1,0:T(8,128)(2,1)S(1)}, u32[]{:S(2)}, u32[]{:S(2)}) %collective-permute-start.87) | collective-permute-done | bytes 1048608 | tf_op jit(solution)/shard_map/ppermute | solution.py:200
  859.4 37.3 %collective-permute-done.93 = bf16[2,2,1,2,1,128,1024]{6,5,4,3,2,1,0:T(8,128)(2,1)S(1)} collective-permute-done((bf16[2,2,1,2,1,128,1024]{6,5,4,3,2,1,0:T(8,128)(2,1)S(1)}, bf16[2,2,1,2,1,128,1024]{6,5,4,3,2,1,0:T(8,128)(2,1)S(1)}, u32[]{:S(2)}, u32[]{:S(2)}) %collective-permute-start.93) | collective-permute-done | bytes 2097184 | tf_op jit(solution)/shard_map/ppermute | solution.py:200
  903.2 15.5 %collective-permute-done.94 = bf16[2,2,1,1,1,128,1024]{6,5,4,3,2,1,0:T(8,128)(2,1)S(1)} collective-permute-done((bf16[2,2,1,1,1,128,1024]{6,5,4,3,2,1,0:T(8,128)(2,1)S(1)}, bf16[2,2,1,1,1,128,1024]{6,5,4,3,2,1,0:T(8,128)(2,1)S(1)}, u32[]{:S(2)}, u32[]{:S(2)}) %collective-permute-start.94) | collective-permute-done | bytes 1048608 | tf_op jit(solution)/shard_map/ppermute | solution.py:200
  925.7 8.1 collective-permute-done.95
  936.8 7.4 collective-permute-done.96
  (572 shorter events, 321.1 us)
Async XLA Ops:
  1.5 48.6 %collective-permute-start.20 = (f32[768]{0:T(1024)S(1)}, f32[768]{0:T(1024)S(1)}, u32[]{:S(2)}, u32[]{:S(2)}) collective-permute-start(f32[768]{0:T(1024)S(1)} %reduce.3), channel_id=1, source_target_pairs={{0,3},{1,2},{2,1},{3,0},{4,7},{5,6},{6,5},{7,4},{8,11},{9,10},{10,... | collective-permute-start | bytes 9224 | tf_op jit(solution)/shard_map/ppermute | solution.py:200
  4.0 46.1 %collective-permute-start.19 = (f32[768]{0:T(1024)S(1)}, f32[768]{0:T(1024)S(1)}, u32[]{:S(2)}, u32[]{:S(2)}) collective-permute-start(f32[768]{0:T(1024)S(1)} %reduce.3), channel_id=1, source_target_pairs={{0,2},{1,3},{2,0},{3,1},{4,6},{5,7},{6,4},{7,5},{8,10},{9,11},{10,... | collective-permute-start | bytes 9224 | tf_op jit(solution)/shard_map/ppermute | solution.py:200
  4.6 48.4 %collective-permute-start.18 = (f32[768]{0:T(1024)S(1)}, f32[768]{0:T(1024)S(1)}, u32[]{:S(2)}, u32[]{:S(2)}) collective-permute-start(f32[768]{0:T(1024)S(1)} %reduce.3), channel_id=1, source_target_pairs={{0,1},{1,0},{2,3},{3,2},{4,5},{5,4},{6,7},{7,6},{8,9},{9,8},{10,11... | collective-permute-start | bytes 9224 | tf_op jit(solution)/shard_map/ppermute | solution.py:200
  5.8 67.4 %collective-permute-start.35 = (bf16[1,1,1,1,1,32,4096]{6,5,4,3,2,1,0:T(8,128)(2,1)S(1)}, bf16[1,1,1,1,1,32,4096]{6,5,4,3,2,1,0:T(8,128)(2,1)S(1)}, u32[]{:S(2)}, u32[]{:S(2)}) collective-permute-start(bf16[1,1,1,1,1,32,4096]{6,5,4,3,2,1,0:T(8,128)(2,1)S(1)} %get-tuple-element.108), channel_id=1, source_target_pairs={{0,16},{4,20},{8,24},{12,28},{16,0},{20,4},{24,8},{28,12},{1,17},{... | collective-permute-start | bytes 786440 | tf_op jit(solution)/shard_map/ppermute | solution.py:200
  9.8 43.2 %collective-permute-start.10 = (bf16[1,1,1,1,1,32,1024]{6,5,4,3,2,1,0:T(8,128)(2,1)S(1)}, bf16[1,1,1,1,1,32,1024]{6,5,4,3,2,1,0:T(8,128)(2,1)S(1)}, u32[]{:S(2)}, u32[]{:S(2)}) collective-permute-start(bf16[1,1,1,1,1,32,1024]{6,5,4,3,2,1,0:T(8,128)(2,1)S(1)} %get-tuple-element.184), channel_id=1, source_target_pairs={{0,16},{4,20},{8,24},{12,28},{16,0},{20,4},{24,8},{28,12},{1,17},{... | collective-permute-start | bytes 196616 | tf_op jit(solution)/shard_map/ppermute | solution.py:200
  128.0 139.5 %collective-permute-start.38 = (bf16[2,2,2,1,1,32,4096]{6,5,4,3,2,1,0:T(8,128)(2,1)}, bf16[2,2,2,1,1,32,4096]{6,5,4,3,2,1,0:T(8,128)(2,1)}, u32[]{:S(2)}, u32[]{:S(2)}) collective-permute-start(bf16[2,2,2,1,1,32,4096]{6,5,4,3,2,1,0:T(8,128)(2,1)} %maximum_select_fusion.9), channel_id=1, source_target_pairs={{0,2},{1,3},{2,0},{3,1},{4,6},{5,7},{6,4},{7,5},{8,10},{9,11},{10,... | collective-permute-start | bytes 6291464 | tf_op jit(solution)/shard_map/ppermute | solution.py:200
  134.6 193.6 %collective-permute-start.43 = (bf16[2,2,1,2,1,128,1024]{6,5,4,3,2,1,0:T(8,128)(2,1)}, bf16[2,2,1,2,1,128,1024]{6,5,4,3,2,1,0:T(8,128)(2,1)}, u32[]{:S(2)}, u32[]{:S(2)}) collective-permute-start(bf16[2,2,1,2,1,128,1024]{6,5,4,3,2,1,0:T(8,128)(2,1)} %maximum_select_fusion.11), channel_id=1, source_target_pairs={{0,4},{4,0},{8,12},{12,8},{16,20},{20,16},{24,28},{28,24},{1,5},{5... | collective-permute-start | bytes 6291464 | tf_op jit(solution)/shard_map/ppermute | solution.py:200
  146.0 52.6 %collective-permute-start.16 = (bf16[768,384]{0,1:T(8,128)(2,1)S(1)}, bf16[768,384]{0,1:T(8,128)(2,1)S(1)}, u32[]{:S(2)}, u32[]{:S(2)}) collective-permute-start(bf16[768,384]{0,1:T(8,128)(2,1)S(1)} %pad_maximum_fusion.10), channel_id=1, source_target_pairs={{0,2},{1,3},{2,0},{3,1},{4,6},{5,7},{6,4},{7,5},{8,10},{9,11},{10,... | collective-permute-start | bytes 1769480 | tf_op jit(solution)/shard_map/ppermute | solution.py:200
  148.7 52.0 %collective-permute-start.15 = (bf16[768,384]{0,1:T(8,128)(2,1)S(1)}, bf16[768,384]{0,1:T(8,128)(2,1)S(1)}, u32[]{:S(2)}, u32[]{:S(2)}) collective-permute-start(bf16[768,384]{0,1:T(8,128)(2,1)S(1)} %pad_maximum_fusion.9), channel_id=1, source_target_pairs={{0,1},{1,0},{2,3},{3,2},{4,5},{5,4},{6,7},{7,6},{8,9},{9,8},{10,11... | collective-permute-start | bytes 1769480 | tf_op jit(solution)/shard_map/ppermute | solution.py:200
  186.7 60.2 %collective-permute-start.26 = (bf16[768,384]{0,1:T(8,128)(2,1)}, bf16[768,384]{0,1:T(8,128)(2,1)}, u32[]{:S(2)}, u32[]{:S(2)}) collective-permute-start(bf16[768,384]{0,1:T(8,128)(2,1)} %pad_maximum_fusion.14), channel_id=1, source_target_pairs={{0,3},{1,2},{2,1},{3,0},{4,7},{5,6},{6,5},{7,4},{8,11},{9,10},{10,... | collective-permute-start | bytes 1769480 | tf_op jit(solution)/shard_map/ppermute | solution.py:200
  198.6 50.9 %collective-permute-start.25 = (bf16[768,384]{0,1:T(8,128)(2,1)}, bf16[768,384]{0,1:T(8,128)(2,1)}, u32[]{:S(2)}, u32[]{:S(2)}) collective-permute-start(bf16[768,384]{0,1:T(8,128)(2,1)} %pad_maximum_fusion.13), channel_id=1, source_target_pairs={{0,2},{1,3},{2,0},{3,1},{4,6},{5,7},{6,4},{7,5},{8,10},{9,11},{10,... | collective-permute-start | bytes 1769480 | tf_op jit(solution)/shard_map/ppermute | solution.py:200
  200.7 51.9 %collective-permute-start.24 = (bf16[768,384]{0,1:T(8,128)(2,1)}, bf16[768,384]{0,1:T(8,128)(2,1)}, u32[]{:S(2)}, u32[]{:S(2)}) collective-permute-start(bf16[768,384]{0,1:T(8,128)(2,1)} %pad_maximum_fusion.12), channel_id=1, source_target_pairs={{0,1},{1,0},{2,3},{3,2},{4,5},{5,4},{6,7},{7,6},{8,9},{9,8},{10,11... | collective-permute-start | bytes 1769480 | tf_op jit(solution)/shard_map/ppermute | solution.py:200
  246.9 64.0 %collective-permute-start.22 = (bf16[768,128]{1,0:T(8,128)(2,1)}, bf16[768,128]{1,0:T(8,128)(2,1)S(1)}, u32[]{:S(2)}, u32[]{:S(2)}) collective-permute-start(bf16[768,128]{1,0:T(8,128)(2,1)} %get-tuple-element.118), channel_id=1, source_target_pairs={{0,2},{1,3},{2,0},{3,1},{4,6},{5,7},{6,4},{7,5},{8,10},{9,11},{10,... | collective-permute-start | bytes 589832 | tf_op jit(solution)/shard_map/ppermute | solution.py:200
  249.5 62.1 %collective-permute-start.23 = (bf16[768,128]{1,0:T(8,128)(2,1)}, bf16[768,128]{1,0:T(8,128)(2,1)S(1)}, u32[]{:S(2)}, u32[]{:S(2)}) collective-permute-start(bf16[768,128]{1,0:T(8,128)(2,1)} %get-tuple-element.117), channel_id=1, source_target_pairs={{0,3},{1,2},{2,1},{3,0},{4,7},{5,6},{6,5},{7,4},{8,11},{9,10},{10,... | collective-permute-start | bytes 589832 | tf_op jit(solution)/shard_map/ppermute | solution.py:200
  252.6 60.0 %collective-permute-start.21 = (bf16[768,128]{1,0:T(8,128)(2,1)}, bf16[768,128]{1,0:T(8,128)(2,1)}, u32[]{:S(2)}, u32[]{:S(2)}) collective-permute-start(bf16[768,128]{1,0:T(8,128)(2,1)} %get-tuple-element.116), channel_id=1, source_target_pairs={{0,1},{1,0},{2,3},{3,2},{4,5},{5,4},{6,7},{7,6},{8,9},{9,8},{10,11... | collective-permute-start | bytes 589832 | tf_op jit(solution)/shard_map/ppermute | solution.py:200
  271.7 61.0 %collective-permute-start.39 = (bf16[2,2,2,2,1,32,4096]{6,5,4,3,2,1,0:T(8,128)(2,1)S(1)}, bf16[2,2,2,2,1,32,4096]{6,5,4,3,2,1,0:T(8,128)(2,1)}, u32[]{:S(2)}, u32[]{:S(2)}) collective-permute-start(bf16[2,2,2,2,1,32,4096]{6,5,4,3,2,1,0:T(8,128)(2,1)S(1)} %maximum_select_fusion.2), channel_id=1, source_target_pairs={{0,1},{1,0},{2,3},{3,2},{4,5},{5,4},{6,7},{7,6},{8,9},{9,8},{10,11... | collective-permute-start | bytes 12582920 | tf_op jit(solution)/shard_map/ppermute | solution.py:200
  332.6 42.4 %collective-permute-start.44 = (bf16[2,2,2,2,1,128,1024]{6,5,4,3,2,1,0:T(8,128)(2,1)S(1)}, bf16[2,2,2,2,1,128,1024]{6,5,4,3,2,1,0:T(8,128)(2,1)}, u32[]{:S(2)}, u32[]{:S(2)}) collective-permute-start(bf16[2,2,2,2,1,128,1024]{6,5,4,3,2,1,0:T(8,128)(2,1)S(1)} %maximum_select_fusion.3), channel_id=1, source_target_pairs={{0,1},{1,0},{2,3},{3,2},{4,5},{5,4},{6,7},{7,6},{8,9},{9,8},{10,11... | collective-permute-start | bytes 12582920 | tf_op jit(solution)/shard_map/ppermute | solution.py:200
  463.3 76.7 %collective-permute-start.53 = (bf16[768,128]{1,0:T(8,128)(2,1)S(1)}, bf16[768,128]{1,0:T(8,128)(2,1)S(1)}, u32[]{:S(2)}, u32[]{:S(2)}) collective-permute-start(bf16[768,128]{1,0:T(8,128)(2,1)S(1)} %get-tuple-element.70), channel_id=1, source_target_pairs={{0,3},{1,2},{2,1},{3,0},{4,7},{5,6},{6,5},{7,4},{8,11},{9,10},{10,... | collective-permute-start | bytes 589832 | tf_op jit(solution)/shard_map/ppermute | solution.py:200
  463.4 77.1 %collective-permute-start.52 = (bf16[768,128]{1,0:T(8,128)(2,1)S(1)}, bf16[768,128]{1,0:T(8,128)(2,1)}, u32[]{:S(2)}, u32[]{:S(2)}) collective-permute-start(bf16[768,128]{1,0:T(8,128)(2,1)S(1)} %get-tuple-element.71), channel_id=1, source_target_pairs={{0,2},{1,3},{2,0},{3,1},{4,6},{5,7},{6,4},{7,5},{8,10},{9,11},{10,... | collective-permute-start | bytes 589832 | tf_op jit(solution)/shard_map/ppermute | solution.py:200
  478.1 62.5 %collective-permute-start.51 = (bf16[768,128]{1,0:T(8,128)(2,1)S(1)}, bf16[768,128]{1,0:T(8,128)(2,1)S(1)}, u32[]{:S(2)}, u32[]{:S(2)}) collective-permute-start(bf16[768,128]{1,0:T(8,128)(2,1)S(1)} %get-tuple-element.72), channel_id=1, source_target_pairs={{0,1},{1,0},{2,3},{3,2},{4,5},{5,4},{6,7},{7,6},{8,9},{9,8},{10,11... | collective-permute-start | bytes 589832 | tf_op jit(solution)/shard_map/ppermute | solution.py:200
  478.1 223.3 %collective-permute-start.78 = (bf16[2,2,2,2,1,32,1024]{6,5,4,3,2,1,0:T(8,128)(2,1)}, bf16[2,2,2,2,1,32,1024]{6,5,4,3,2,1,0:T(8,128)(2,1)}, u32[]{:S(2)}, u32[]{:S(2)}) collective-permute-start(bf16[2,2,2,2,1,32,1024]{6,5,4,3,2,1,0:T(8,128)(2,1)} %constant_dynamic-slice_fusion.14), channel_id=1, source_target_pairs={{0,1},{1,0},{2,3},{3,2},{4,5},{5,4},{6,7},{7,6},{8,9},{9,8},{10,11... | collective-permute-start | bytes 3145736 | tf_op jit(solution)/shard_map/ppermute | solution.py:200
  478.6 297.8 %collective-permute-start.85 = (bf16[2,2,2,2,1,32,4096]{6,5,4,3,2,1,0:T(8,128)(2,1)}, bf16[2,2,2,2,1,32,4096]{6,5,4,3,2,1,0:T(8,128)(2,1)}, u32[]{:S(2)}, u32[]{:S(2)}) collective-permute-start(bf16[2,2,2,2,1,32,4096]{6,5,4,3,2,1,0:T(8,128)(2,1)} %constant_dynamic-slice_fusion.9), channel_id=1, source_target_pairs={{0,1},{1,0},{2,3},{3,2},{4,5},{5,4},{6,7},{7,6},{8,9},{9,8},{10,11... | collective-permute-start | bytes 12582920 | tf_op jit(solution)/shard_map/ppermute | solution.py:200
  540.0 63.9 %collective-permute-start.48 = (bf16[768,384]{1,0:T(8,128)(2,1)S(1)}, bf16[768,384]{1,0:T(8,128)(2,1)S(1)}, u32[]{:S(2)}, u32[]{:S(2)}) collective-permute-start(bf16[768,384]{1,0:T(8,128)(2,1)S(1)} %get-tuple-element.66), channel_id=1, source_target_pairs={{0,1},{1,0},{2,3},{3,2},{4,5},{5,4},{6,7},{7,6},{8,9},{9,8},{10,11... | collective-permute-start | bytes 1769480 | tf_op jit(solution)/shard_map/ppermute | solution.py:200
  540.5 63.6 %collective-permute-start.50 = (bf16[768,384]{1,0:T(8,128)(2,1)S(1)}, bf16[768,384]{1,0:T(8,128)(2,1)S(1)}, u32[]{:S(2)}, u32[]{:S(2)}) collective-permute-start(bf16[768,384]{1,0:T(8,128)(2,1)S(1)} %get-tuple-element.67), channel_id=1, source_target_pairs={{0,3},{1,2},{2,1},{3,0},{4,7},{5,6},{6,5},{7,4},{8,11},{9,10},{10,... | collective-permute-start | bytes 1769480 | tf_op jit(solution)/shard_map/ppermute | solution.py:200
  540.6 64.0 %collective-permute-start.49 = (bf16[768,384]{1,0:T(8,128)(2,1)S(1)}, bf16[768,384]{1,0:T(8,128)(2,1)S(1)}, u32[]{:S(2)}, u32[]{:S(2)}) collective-permute-start(bf16[768,384]{1,0:T(8,128)(2,1)S(1)} %get-tuple-element.68), channel_id=1, source_target_pairs={{0,2},{1,3},{2,0},{3,1},{4,6},{5,7},{6,4},{7,5},{8,10},{9,11},{10,... | collective-permute-start | bytes 1769480 | tf_op jit(solution)/shard_map/ppermute | solution.py:200
  606.8 223.9 %collective-permute-start.92 = (bf16[2,2,2,2,1,128,1024]{6,5,4,3,2,1,0:T(8,128)(2,1)}, bf16[2,2,2,2,1,128,1024]{6,5,4,3,2,1,0:T(8,128)(2,1)}, u32[]{:S(2)}, u32[]{:S(2)}) collective-permute-start(bf16[2,2,2,2,1,128,1024]{6,5,4,3,2,1,0:T(8,128)(2,1)} %constant_dynamic-slice_fusion.4), channel_id=1, source_target_pairs={{0,1},{1,0},{2,3},{3,2},{4,5},{5,4},{6,7},{7,6},{8,9},{9,8},{10,11... | collective-permute-start | bytes 12582920 | tf_op jit(solution)/shard_map/ppermute | solution.py:200
  653.1 70.9 %collective-permute-start.71 = (bf16[2,2,2,2,1,32,1024]{6,5,4,3,2,1,0:T(8,128)(2,1)}, bf16[2,2,2,2,1,32,1024]{6,5,4,3,2,1,0:T(8,128)(2,1)}, u32[]{:S(2)}, u32[]{:S(2)}) collective-permute-start(bf16[2,2,2,2,1,32,1024]{6,5,4,3,2,1,0:T(8,128)(2,1)} %constant_dynamic-slice_fusion.20), channel_id=1, source_target_pairs={{0,1},{1,0},{2,3},{3,2},{4,5},{5,4},{6,7},{7,6},{8,9},{9,8},{10,11... | collective-permute-start | bytes 3145736 | tf_op jit(solution)/shard_map/ppermute | solution.py:200
  655.4 76.2 %collective-permute-start.64 = (bf16[2,2,2,2,1,32,1024]{6,5,4,3,2,1,0:T(8,128)(2,1)}, bf16[2,2,2,2,1,32,1024]{6,5,4,3,2,1,0:T(8,128)(2,1)}, u32[]{:S(2)}, u32[]{:S(2)}) collective-permute-start(bf16[2,2,2,2,1,32,1024]{6,5,4,3,2,1,0:T(8,128)(2,1)} %constant_dynamic-slice_fusion.25), channel_id=1, source_target_pairs={{0,1},{1,0},{2,3},{3,2},{4,5},{5,4},{6,7},{7,6},{8,9},{9,8},{10,11... | collective-permute-start | bytes 3145736 | tf_op jit(solution)/shard_map/ppermute | solution.py:200
  780.4 48.6 %collective-permute-start.86 = (bf16[2,2,2,1,1,32,4096]{6,5,4,3,2,1,0:T(8,128)(2,1)S(1)}, bf16[2,2,2,1,1,32,4096]{6,5,4,3,2,1,0:T(8,128)(2,1)S(1)}, u32[]{:S(2)}, u32[]{:S(2)}) collective-permute-start(bf16[2,2,2,1,1,32,4096]{6,5,4,3,2,1,0:T(8,128)(2,1)S(1)} %constant_dynamic-slice_fusion.8), channel_id=1, source_target_pairs={{0,2},{1,3},{2,0},{3,1},{4,6},{5,7},{6,4},{7,5},{8,10},{9,11},{10,... | collective-permute-start | bytes 6291464 | tf_op jit(solution)/shard_map/ppermute | solution.py:200
  794.5 42.4 %collective-permute-start.76 = (bf16[1,1,1,1,1,32,1024]{6,5,4,3,2,1,0:T(8,128)(2,1)S(1)}, bf16[1,1,1,1,1,32,1024]{6,5,4,3,2,1,0:T(8,128)(2,1)S(1)}, u32[]{:S(2)}, u32[]{:S(2)}) collective-permute-start(bf16[1,1,1,1,1,32,1024]{6,5,4,3,2,1,0:T(8,128)(2,1)S(1)} %add_convert_fusion.32), channel_id=1, source_target_pairs={{0,2},{1,3},{2,0},{3,1},{4,6},{5,7},{6,4},{7,5},{8,10},{9,11},{10,... | collective-permute-start | bytes 196616 | tf_op jit(solution)/shard_map/ppermute | solution.py:200
  835.4 61.3 %collective-permute-start.93 = (bf16[2,2,1,2,1,128,1024]{6,5,4,3,2,1,0:T(8,128)(2,1)S(1)}, bf16[2,2,1,2,1,128,1024]{6,5,4,3,2,1,0:T(8,128)(2,1)S(1)}, u32[]{:S(2)}, u32[]{:S(2)}) collective-permute-start(bf16[2,2,1,2,1,128,1024]{6,5,4,3,2,1,0:T(8,128)(2,1)S(1)} %constant_dynamic-slice_fusion.3), channel_id=1, source_target_pairs={{0,4},{4,0},{8,12},{12,8},{16,20},{20,16},{24,28},{28,24},{1,5},{5... | collective-permute-start | bytes 6291464 | tf_op jit(solution)/shard_map/ppermute | solution.py:200
  856.5 43.1 %collective-permute-start.88 = (bf16[2,1,1,1,1,32,4096]{6,5,4,3,2,1,0:T(8,128)(2,1)S(1)}, bf16[2,1,1,1,1,32,4096]{6,5,4,3,2,1,0:T(8,128)(2,1)S(1)}, u32[]{:S(2)}, u32[]{:S(2)}) collective-permute-start(bf16[2,1,1,1,1,32,4096]{6,5,4,3,2,1,0:T(8,128)(2,1)S(1)} %constant_dynamic-slice_fusion.6), channel_id=1, source_target_pairs={{0,8},{4,12},{8,0},{12,4},{16,24},{20,28},{24,16},{28,20},{1,9},{5... | collective-permute-start | bytes 1572872 | tf_op jit(solution)/shard_map/ppermute | solution.py:200
  (136 other events, 1805.2 us)
